TPU v7x, 256 devices: a whole 4x4x8 slice. The times are simulated.
256 devices in a mesh: row: 16 (over z, core), col: 16 (over y, x).
Axes of the slice: x: 4, y: 4, z: 8, core: 2. Of those that a mesh axis runs over, the one named last changes fastest.
Arguments:
- features: bfloat16 [131072, 256], P(('col', 'row')), may hold values from -0.0625 to 0.0625
- weight: bfloat16 [256, 256], replicated, may hold values from -0.375 to 0.375
- pre_act: bfloat16 [131072, 256], P('row', 'col'), may hold values from -6 to 6
- grad_out: bfloat16 [131072, 256], P('row', 'col'), may hold values from -6 to 6
- tile_ids: int32 [16, 16, 320], P('row', 'col'), may hold values from 0 to 4095, as said below
- tile_count: int32 [16, 16], P('row', 'col'), may hold values from 1 to 320
- tile_values: bfloat16 [16, 16, 320, 128, 128], P('row', 'col'), may hold values from -0.078125 to 0.078125
Outputs:
- grad_in: bfloat16 [131072, 256], P(('col', 'row'))
- grad_weight: float32 [256, 256], P('row', 'col')
Inputs may be any that keep to these rules, and one draw needn't show every extreme that they name: `tile_ids`: the entries of one grid cell's list are distinct; slots from tile_count on are not used.
All inputs are finite; a program needn't handle non-finite values.
Results may differ from a plain program's by a relative error of at most 0.005.
Values may be sent and summed in bfloat16 or wider, within the bound.
No kernel may reach another device: no remote copies, remote signals or barrier semaphores. Data moves between devices by JAX's collectives and lax.ppermute only.
A program may use at most 128 MiB of HBM per device.

v0:
```python
import math

import jax
import jax.numpy as jnp
from jax import lax
from jax.sharding import PartitionSpec as P


def per_device(features, weight, pre_act, grad_out, tile_ids, tile_count, tile_values):
    grad_pre = jnp.where(pre_act > 0, grad_out, jnp.zeros_like(grad_out))
    gathered = lax.all_gather(grad_pre, "col", axis=1, tiled=True)
    feat_width = gathered.shape[1]
    row_tiles = gathered.shape[0] // 128
    node_rows = features.shape[0]
    col_tiles = node_rows // 128 * lax.axis_size("row")
    source = gathered.reshape(row_tiles, 128, feat_width)
    tile_list = tile_ids[0, 0]
    values = tile_values[0, 0]
    live_tiles = tile_count[0, 0]
    capacity = tile_list.shape[0]
    stride = math.gcd(capacity, 64)

    def add_block(block_index, running):
        first_slot = block_index * stride
        block_list = lax.dynamic_slice_in_dim(tile_list, first_slot, stride, 0)
        block_values = lax.dynamic_slice_in_dim(values, first_slot, stride, 0)
        is_live = first_slot + jnp.arange(stride, dtype=jnp.int32) < live_tiles
        picked = source[block_list // col_tiles]
        product = jnp.einsum(
            "tkn,tkf->tnf", block_values, picked, preferred_element_type=jnp.float32
        )
        product = jnp.where(is_live[:, None, None], product, jnp.zeros_like(product))
        return running.at[block_list % col_tiles].add(product)

    block_steps = capacity // stride
    start_sum = jnp.zeros((col_tiles, 128, feat_width), jnp.float32)
    summed = lax.fori_loop(0, block_steps, add_block, start_sum)
    partial_value = summed.reshape(col_tiles * 128, feat_width)
    spread = lax.psum_scatter(partial_value, "row", scatter_dimension=0, tiled=True).astype(
        jnp.bfloat16
    )
    grad_in = lax.dot_general(
        spread, weight, (((1,), (1,)), ((), ())), preferred_element_type=jnp.float32
    ).astype(jnp.bfloat16)
    weight_term = lax.dot_general(
        features, spread, (((0,), (0,)), ((), ())), preferred_element_type=jnp.float32
    )
    whole_sum = lax.psum(weight_term, ("row", "col"))
    height = weight_term.shape[0] // lax.axis_size("row")
    breadth = weight_term.shape[1] // lax.axis_size("col")
    grad_weight = lax.dynamic_slice(
        whole_sum,
        (lax.axis_index("row") * height, lax.axis_index("col") * breadth),
        (height, breadth),
    )
    return (grad_in, grad_weight)


def solution(mesh):
    return jax.shard_map(
        per_device,
        mesh=mesh,
        in_specs=(
            P(("col", "row"), None),
            P(),
            P("row", "col"),
            P("row", "col"),
            P("row", "col", None),
            P("row", "col"),
            P("row", "col", None, None, None),
        ),
        out_specs=(P(("col", "row"), None), P("row", "col")),
        check_vma=False,
    )
```

profile of v0, /device:TPU:1, one launch (start us, length us, event | category | flops | bytes accessed | tf_op | source)
XLA Modules:
  0.0 577.2 jit_solution(13152827750049041143)
XLA Ops:
  7.2 1.8 compare_select_fusion.5
  9.1 0.7 reduce
  9.8 14.4 %copy.9 = bf16[1,1,320,128,128]{3,4,2,1,0:T(8,128)(2,1)} copy(bf16[1,1,320,128,128]{4,3,2,1,0:T(8,128)(2,1)} %param.15) | data formatting | bytes 20971520 | tf_op args[6]
  24.2 47.2 %all-gather.2.cloned.1.call-done = bf16[8192,256]{0,1:T(8,128)(2,1)} async-done(((bf16[8192,16]{0,1:T(8,128)(2,1)}), bf16[8192,256]{0,1:T(8,128)(2,1)}) %all-gather.2.cloned.1.call-update) | async-done | bytes 4194320 | tf_op jit(solution)/shard_map/all_gather | solution.py:11
  71.4 6.4 %copy.10 = bf16[8192,256]{1,0:T(8,128)(2,1)} copy(bf16[8192,256]{0,1:T(8,128)(2,1)} %all-gather.2.cloned.1.call-done) | data formatting | bytes 8388608 | tf_op jit(solution)/shard_map/all_gather | solution.py:11
  77.8 4.4 broadcast.84
  82.1 163.6 %while.15 = (s32[]{:T(128)}, f32[64,128,256]{2,1,0:T(8,128)}, s32[320]{0:T(512)S(1)}, s32[]{:T(128)}, bf16[320,128,128]{1,2,0:T(8,128)(2,1)}, /*index=5*/bf16[64...) while((s32[]{:T(128)}, f32[64,128,256]{2,1,0:T(8,128)}, s32[320]{0:T(512)S(1)}, ...), condition=%wide.region_2.3_spmd, body=%wide.region_0.2_spmd.sunk | while | flops 541068032 | bytes 48240936 | solution.py:37
  82.2 0.7 add_compare_fusion.2
  82.9 5.0 gather_fusion
  87.9 7.4 %broadcast_select_fusion.2 = f32[64,128,256]{2,1,0:T(8,128)} fusion(pred[64]{0:T(512)(128)(4,1)S(1)} %add_compare_fusion.2, bf16[64,128,256]{2,1,0:T(8,128)(2,1)} %gather_fusion, bf16[320,128,128]{1,2,0:T(8,128)(2,1)} %get-tuple-element.241, s32[]{:T(128)S(6)} %select_n.108), kind=kOutput, calls=%fused_computation.2.clone.1 | convolution fusion | flops 538968064 | bytes 14680132 | tf_op jit(solution)/shard_map/while/body/eval_jaxpr/tkn,tkf->tnf/dot_general | solution.py:29
  95.3 19.5 %scatter_fusion = f32[64,128,256]{2,1,0:T(8,128)} fusion(f32[64,128,256]{2,1,0:T(8,128)} %get-tuple-element.228, s32[64]{0:T(128)S(1)} %compare_select_fusion.10, f32[64,128,256]{2,1,0:T(8,128)} %broadcast_select_fusion.2), kind=kCustom, calls=%fused_computation.1.clone.1 | custom fusion | flops 2097152 | bytes 25166080 | tf_op jit(solution)/shard_map/while/body/eval_jaxpr/scatter-add | solution.py:33
  114.9 0.7 add_compare_fusion.2
  115.5 5.0 gather_fusion
  120.5 7.4 %broadcast_select_fusion.2 = f32[64,128,256]{2,1,0:T(8,128)} fusion(pred[64]{0:T(512)(128)(4,1)S(1)} %add_compare_fusion.2, bf16[64,128,256]{2,1,0:T(8,128)(2,1)} %gather_fusion, bf16[320,128,128]{1,2,0:T(8,128)(2,1)} %get-tuple-element.241, s32[]{:T(128)S(6)} %select_n.108), kind=kOutput, calls=%fused_computation.2.clone.1 | convolution fusion | flops 538968064 | bytes 14680132 | tf_op jit(solution)/shard_map/while/body/eval_jaxpr/tkn,tkf->tnf/dot_general | solution.py:29
  127.9 19.6 %scatter_fusion = f32[64,128,256]{2,1,0:T(8,128)} fusion(f32[64,128,256]{2,1,0:T(8,128)} %get-tuple-element.228, s32[64]{0:T(128)S(1)} %compare_select_fusion.10, f32[64,128,256]{2,1,0:T(8,128)} %broadcast_select_fusion.2), kind=kCustom, calls=%fused_computation.1.clone.1 | custom fusion | flops 2097152 | bytes 25166080 | tf_op jit(solution)/shard_map/while/body/eval_jaxpr/scatter-add | solution.py:33
  148.3 5.0 gather_fusion
  153.2 7.4 %broadcast_select_fusion.2 = f32[64,128,256]{2,1,0:T(8,128)} fusion(pred[64]{0:T(512)(128)(4,1)S(1)} %add_compare_fusion.2, bf16[64,128,256]{2,1,0:T(8,128)(2,1)} %gather_fusion, bf16[320,128,128]{1,2,0:T(8,128)(2,1)} %get-tuple-element.241, s32[]{:T(128)S(6)} %select_n.108), kind=kOutput, calls=%fused_computation.2.clone.1 | convolution fusion | flops 538968064 | bytes 14680132 | tf_op jit(solution)/shard_map/while/body/eval_jaxpr/tkn,tkf->tnf/dot_general | solution.py:29
  160.6 19.8 %scatter_fusion = f32[64,128,256]{2,1,0:T(8,128)} fusion(f32[64,128,256]{2,1,0:T(8,128)} %get-tuple-element.228, s32[64]{0:T(128)S(1)} %compare_select_fusion.10, f32[64,128,256]{2,1,0:T(8,128)} %broadcast_select_fusion.2), kind=kCustom, calls=%fused_computation.1.clone.1 | custom fusion | flops 2097152 | bytes 25166080 | tf_op jit(solution)/shard_map/while/body/eval_jaxpr/scatter-add | solution.py:33
  180.5 0.7 add_compare_fusion.2
  181.2 5.0 gather_fusion
  186.1 7.4 %broadcast_select_fusion.2 = f32[64,128,256]{2,1,0:T(8,128)} fusion(pred[64]{0:T(512)(128)(4,1)S(1)} %add_compare_fusion.2, bf16[64,128,256]{2,1,0:T(8,128)(2,1)} %gather_fusion, bf16[320,128,128]{1,2,0:T(8,128)(2,1)} %get-tuple-element.241, s32[]{:T(128)S(6)} %select_n.108), kind=kOutput, calls=%fused_computation.2.clone.1 | convolution fusion | flops 538968064 | bytes 14680132 | tf_op jit(solution)/shard_map/while/body/eval_jaxpr/tkn,tkf->tnf/dot_general | solution.py:29
  193.5 19.5 %scatter_fusion = f32[64,128,256]{2,1,0:T(8,128)} fusion(f32[64,128,256]{2,1,0:T(8,128)} %get-tuple-element.228, s32[64]{0:T(128)S(1)} %compare_select_fusion.10, f32[64,128,256]{2,1,0:T(8,128)} %broadcast_select_fusion.2), kind=kCustom, calls=%fused_computation.1.clone.1 | custom fusion | flops 2097152 | bytes 25166080 | tf_op jit(solution)/shard_map/while/body/eval_jaxpr/scatter-add | solution.py:33
  213.1 0.7 add_compare_fusion.2
  213.8 5.0 gather_fusion
  218.8 7.4 %broadcast_select_fusion.2 = f32[64,128,256]{2,1,0:T(8,128)} fusion(pred[64]{0:T(512)(128)(4,1)S(1)} %add_compare_fusion.2, bf16[64,128,256]{2,1,0:T(8,128)(2,1)} %gather_fusion, bf16[320,128,128]{1,2,0:T(8,128)(2,1)} %get-tuple-element.241, s32[]{:T(128)S(6)} %select_n.108), kind=kOutput, calls=%fused_computation.2.clone.1 | convolution fusion | flops 538968064 | bytes 14680132 | tf_op jit(solution)/shard_map/while/body/eval_jaxpr/tkn,tkf->tnf/dot_general | solution.py:29
  226.2 19.6 %scatter_fusion = f32[64,128,256]{2,1,0:T(8,128)} fusion(f32[64,128,256]{2,1,0:T(8,128)} %get-tuple-element.228, s32[64]{0:T(128)S(1)} %compare_select_fusion.10, f32[64,128,256]{2,1,0:T(8,128)} %broadcast_select_fusion.2), kind=kCustom, calls=%fused_computation.1.clone.1 | custom fusion | flops 2097152 | bytes 25166080 | tf_op jit(solution)/shard_map/while/body/eval_jaxpr/scatter-add | solution.py:33
  245.8 67.3 %reduce-scatter.2.cloned.1.call-done = f32[512,256]{1,0:T(8,128)} async-done(((f32[8192,256]{1,0:T(8,128)}), f32[512,256]{1,0:T(8,128)}) %reduce-scatter.2.cloned.1.call-update) | async-done | bytes 524304 | tf_op jit(solution)/shard_map/reduce_scatter | solution.py:39
  313.1 2.0 convolution_bitcast_fusion
  315.2 2.0 convolution_convert_fusion
  317.2 252.0 %all-reduce.2.cloned.1.call-done = f32[256,256]{0,1:T(8,128)} async-done(((f32[256,256]{0,1:T(8,128)}), f32[256,256]{0,1:T(8,128)}) %all-reduce.2.cloned.1.call-update) | async-done | bytes 262160 | tf_op jit(solution)/shard_map/psum | solution.py:48
  569.2 0.8 dynamic_slice.23
  570.0 0.7 copy.11
  (26 shorter events, 1.3 us)
Async XLA Ops:
  7.2 306.0 %copy-start = (bf16[512,256]{1,0:T(8,128)(2,1)S(1)}, bf16[512,256]{1,0:T(8,128)(2,1)}, u32[]{:S(2)}) copy-start(bf16[512,256]{1,0:T(8,128)(2,1)} %param.9) | copy-start | bytes 786436
  7.2 64.2 %all-gather.2.cloned.1.call-start = ((), (), s32[]{:S(2)}) async-start(), calls=%async_computation.1 | async-start | bytes 4456448 | tf_op jit(solution)/shard_map/all_gather | solution.py:11
  9.0 304.1 %reduce-scatter.2.cloned.1.call-start = ((), (), s32[]{:S(2)}) async-start(), calls=%async_computation.2 | async-start | bytes 8912896 | tf_op jit(solution)/shard_map/reduce_scatter | solution.py:39
  245.7 69.5 %copy-start.1 = (bf16[256,256]{1,0:T(8,128)(2,1)S(1)}, bf16[256,256]{1,0:T(8,128)(2,1)}, u32[]{:S(2)}) copy-start(bf16[256,256]{1,0:T(8,128)(2,1)} %param.10) | copy-start | bytes 393220
  245.8 323.4 %all-reduce.2.cloned.1.call-start = ((), (), s32[]{:S(2)}) async-start(), calls=%async_computation.3 | async-start | bytes 524288 | tf_op jit(solution)/shard_map/psum | solution.py:48
Sparse Core Ops, SparseCore 0:
  11.0 60.3 all-gather.1
  245.9 67.2 reduce-scatter.1
  318.6 250.5 all-reduce.1
where the time goes:
time: 579 us; the launch traced here: 577 us
  waiting for transfers between devices  367 us (63%)
  other arithmetic  104 us (18%)
  local copies, waits for them, and re-layouts  51.4 us (9%)
  matrix products  41 us (7%)
  between operations  13.8 us (2%)
    psum x1, waiting for transfers between devices, per_device(): whole_sum = lax.psum(weight_term, ('row', 'col'))  252 us
    scatter-add x5, other arithmetic, add_block(): return running.at[block_list % col_tiles].add(product)  98 us
    reduce_scatter x1, waiting for transfers between devices, per_device(): lax.psum_scatter(partial_value, 'row', scatter_dimension=0, tiled=True)  67.3 us
    all_gather x1, waiting for transfers between devices, per_device(): gathered = lax.all_gather(grad_pre, 'col', axis=1, tiled=True)  47.2 us
    dot_general x5, matrix products, add_block(): jnp.einsum('tkn,tkf->tnf', block_values, picked, preferred_element_type=j...  37 us
    gather x5, local copies, waits for them, and re-layouts, add_block(): picked = source[block_list // col_tiles]  24.8 us
    unnamed x6, local copies, waits for them, and re-layouts  15.1 us
  transfers between devices with their start and end apart: 3, of which 3 were waited for; matrix products, arithmetic and copies ran while one was open for 3% of the time, Pallas kernels for 0%

commit v1 on v0

v1 whole, which is shorter than its diff:
```python
import functools

import jax
import jax.numpy as jnp
from jax import lax
from jax.experimental import pallas as pl
from jax.experimental.pallas import tpu as pltpu
from jax.sharding import PartitionSpec as P

BF = jnp.bfloat16
F32 = jnp.float32
TILE = 128
NX = 4
NY = 4
NZ = 8
COLS = 64
STAGES = 4
STAGE_COLS = COLS // STAGES
GROUP = 4
VMEM_LIMIT = 24 * 1024 * 1024


def shift_x(array, step):
    pairs = [(i, (i // NX) * NX + (i % NX + step) % NX) for i in range(NX * NY)]
    return lax.ppermute(array, "col", pairs)


def shift_y(array, step):
    pairs = [(i, (i + NX * step) % (NX * NY)) for i in range(NX * NY)]
    return lax.ppermute(array, "col", pairs)


def shift_z(array, step):
    pairs = [(i, (i + 2 * step) % (2 * NZ)) for i in range(2 * NZ)]
    return lax.ppermute(array, "row", pairs)


def swap_core(array):
    return lax.ppermute(array, "row", [(i, i ^ 1) for i in range(2 * NZ)])


def line_by_hops(shift, block):
    ahead, behind = shift(block, -1), shift(block, 1)
    half = block.shape[0] // 2
    return block, ahead, shift(behind[:half], 1), shift(ahead[half:], -1), behind


def line(shift, block):
    return block, shift(block, -1), shift(block, 2), shift(block, 1)


def pair_kernel(ids_ref, count_ref, info_ref, values_hbm, table_ref, values_ref, value_sem):
    copy = pltpu.make_async_copy(values_hbm, values_ref, value_sem)
    copy.start()
    slots = ids_ref.shape[1]
    room = table_ref.shape[1]
    ids = jnp.broadcast_to(ids_ref[...], (8, slots))
    slot = lax.broadcasted_iota(jnp.int32, (8, slots), 1)
    live = slot < count_ref[0, 0]
    j = ids & (COLS - 1)
    i = lax.shift_right_logical(ids, 6) & (COLS - 1)
    ahead = (lax.shift_right_logical(j, 3) - info_ref[0]) & (NZ - 1)
    is_right = (ahead >= 1) & (ahead <= 4)
    stage = jnp.where(is_right, 4 - ahead, 3 - ((NZ - ahead) & (NZ - 1)))
    rank = stage * STAGE_COLS + jnp.where(is_right, 0, 8) + (j & 7)
    rank = jnp.where(live, rank, -1)

    def flag(mask):
        return jnp.where(mask, 1.0, 0.0).astype(BF)

    def dot(left, right):
        return jnp.dot(left, right, preferred_element_type=F32)

    columns = lax.broadcasted_iota(jnp.int32, (COLS, slots), 0)
    member = columns == rank[:1]
    before = flag(
        lax.broadcasted_iota(jnp.int32, (slots, slots), 0)
        < lax.broadcasted_iota(jnp.int32, (slots, slots), 1)
    )
    earlier = dot(flag(member), before)
    size = jnp.sum(member.astype(F32), axis=1, keepdims=True)
    pairs = jnp.floor((size + 1.0) * 0.5)
    lower = flag(
        lax.broadcasted_iota(jnp.int32, (COLS, COLS), 1)
        < lax.broadcasted_iota(jnp.int32, (COLS, COLS), 0)
    )
    start = dot(lower, jnp.broadcast_to(pairs, (COLS, TILE)).astype(BF))
    spot = jnp.sum(
        jnp.where(member, earlier + 2.0 * start[:, :1], 0.0), axis=0, keepdims=True
    )
    spot = jnp.where(live[:1], spot, -1.0)
    spot = jnp.broadcast_to(spot, (TILE, slots)).T[:, :1]
    target = 2 * lax.broadcasted_iota(jnp.int32, (slots, room), 1)
    row = lax.broadcasted_iota(jnp.int32, (8, slots), 0)
    facts = jnp.where(row == 0, slot // 16, 0)
    facts = jnp.where(row == 1, slot % 16, facts)
    facts = jnp.where(row == 2, i, facts)
    facts = jnp.where(row == 3, rank & (STAGE_COLS - 1), facts)
    facts = jnp.where(row == 4, 1, facts).astype(F32).astype(BF)
    first = dot(facts, flag(spot == target.astype(F32)))
    second = dot(facts, flag(spot == (target + 1).astype(F32)))

    def code(found):
        return ((found[0:1] * 16.0 + found[1:2]) * COLS + found[2:3]).astype(jnp.int32)

    table_ref[0:1] = code(first)
    table_ref[1:2] = jnp.where(second[4:5] > 0.5, code(second), -1)
    table_ref[2:3] = first[3:4].astype(jnp.int32)
    table_ref[3:4] = jnp.zeros((1, room), jnp.int32)
    table_ref[3:4, :COLS] = start.T[0:1].astype(jnp.int32)
    total = jnp.sum(pairs, axis=0, keepdims=True).astype(jnp.int32)
    table_ref[3:4, TILE : 2 * TILE] = jnp.broadcast_to(total, (1, TILE))
    copy.wait()


def list_pairs(tile_ids, tile_count, info, values):
    smem = pl.BlockSpec(memory_space=pltpu.SMEM)
    vmem = pl.BlockSpec(memory_space=pltpu.VMEM)
    room = 256
    return pl.pallas_call(
        pair_kernel,
        in_specs=[vmem, smem, smem, pl.BlockSpec(memory_space=pl.ANY)],
        out_specs=[vmem, vmem],
        out_shape=[
            jax.ShapeDtypeStruct((4, room), jnp.int32),
            jax.ShapeDtypeStruct(values.shape, BF),
        ],
        scratch_shapes=[pltpu.SemaphoreType.DMA],
        compiler_params=pltpu.CompilerParams(vmem_limit_bytes=16 * 1024 * 1024),
        cost_estimate=pl.CostEstimate(flops=0, bytes_accessed=14_000_000, transcendentals=0),
    )(
        tile_ids.reshape(1, -1),
        tile_count,
        info,
        pltpu.with_memory_space_constraint(values, pltpu.HBM),
    )


def tile_kernel(stage, table_ref, info_ref, *refs):
    *pieces, values_ref, mine_ref, other_ref, acc_ref = refs
    core = info_ref[1]
    width = acc_ref.shape[1]
    begin = table_ref[3, stage * STAGE_COLS]
    end = table_ref[3, (stage + 1) * STAGE_COLS if stage < STAGES - 1 else TILE]

    def clear(j, carry):
        acc_ref[j] = jnp.zeros(acc_ref.shape[1:], F32)
        return carry

    lax.fori_loop(0, STAGE_COLS, clear, 0)

    def gathered(code):
        lanes = pl.ds(pl.multiple_of((code & (COLS - 1)) * TILE, TILE), TILE)
        return jnp.concatenate([piece[:, lanes] for piece in pieces], axis=0)

    def group(g, carry):
        for u in range(GROUP):
            pair = begin + g * GROUP + u
            one, two = table_ref[0, pair], table_ref[1, pair]
            both = two >= 0
            two = jnp.maximum(two, 0)
            left_two = jnp.where(both, gathered(two), jnp.zeros((width, TILE), BF))
            left = jnp.concatenate([gathered(one), left_two], axis=1)
            right = jnp.concatenate(
                [
                    values_ref[lax.shift_right_logical(one, 6)],
                    values_ref[lax.shift_right_logical(two, 6)],
                ],
                axis=0,
            )
            dest = jnp.where(pair < end, table_ref[2, pair], STAGE_COLS)
            acc_ref[dest] += jnp.dot(left, right, preferred_element_type=F32)
        return carry

    lax.fori_loop(0, (end - begin + GROUP - 1) // GROUP, group, 0)

    for side in range(2):
        for q in range(4):
            lanes = slice(q * TILE, (q + 1) * TILE)
            mine_ref[side, :, lanes] = acc_ref[side * 8 + core * 4 + q].astype(BF)
            other_ref[side, :, lanes] = acc_ref[side * 8 + (1 - core) * 4 + q].astype(BF)


def tile_products(stage, table, info, pieces, values):
    width = sum(piece.shape[0] for piece in pieces)
    smem = pl.BlockSpec(memory_space=pltpu.SMEM)
    vmem = pl.BlockSpec(memory_space=pltpu.VMEM)
    return pl.pallas_call(
        functools.partial(tile_kernel, stage),
        in_specs=[smem] * 2 + [vmem] * (len(pieces) + 1),
        out_specs=[vmem] * 2,
        scratch_shapes=[pltpu.VMEM((STAGE_COLS + 1, width, TILE), F32)],
        out_shape=[jax.ShapeDtypeStruct((2, width, 512), BF)] * 2,
        compiler_params=pltpu.CompilerParams(vmem_limit_bytes=VMEM_LIMIT),
        cost_estimate=pl.CostEstimate(flops=0, bytes_accessed=1_000_000, transcendentals=0),
    )(table, info, *pieces, values)


def add_bf(*terms):
    return sum(term.astype(F32) for term in terms).astype(BF)


def final_kernel(
    right_ref, left_ref, mine_ref, other_ref, order_ref, weight_ref, feat_ref, grad_ref, term_ref
):
    held = right_ref[...].astype(F32) + left_ref[...].astype(F32)
    held = held + mine_ref[1].astype(F32) + other_ref[1].astype(F32)
    spread = lax.dot_general(
        order_ref[...], held.astype(BF), (((1,), (0,)), ((), ())), preferred_element_type=F32
    ).astype(BF)
    grad_ref[...] = lax.dot_general(
        spread, weight_ref[...], (((0,), (1,)), ((), ())), preferred_element_type=F32
    ).astype(BF)
    term = lax.dot_general(
        feat_ref[...], spread, (((0,), (1,)), ((), ())), preferred_element_type=F32
    )
    rows = lax.broadcasted_iota(jnp.int32, (8, TILE), 0)
    spans = lax.broadcasted_iota(jnp.int32, (8, TILE), 1) // 16
    for half in range(2):
        part = term[:, half * TILE : (half + 1) * TILE].reshape(32, 8, TILE)
        moved = jnp.zeros_like(part)
        for step in range(8):
            turned = part
            if step:
                turned = pltpu.roll(pltpu.roll(part, 8 - step, 1), 16 * step, 2)
            keep = ((spans - rows) & 7) == step
            moved = jnp.where(keep[None], turned, moved)
        for r in range(16):
            for upper in range(2):
                term_ref[
                    r * 16 + half * 8 : r * 16 + half * 8 + 8, upper * TILE : (upper + 1) * TILE
                ] = moved[2 * r + upper]


def finish(right, left, mine, other, order, weight, features):
    return pl.pallas_call(
        final_kernel,
        out_shape=[
            jax.ShapeDtypeStruct(features.shape, BF),
            jax.ShapeDtypeStruct((256, 256), F32),
        ],
        compiler_params=pltpu.CompilerParams(vmem_limit_bytes=16 * 1024 * 1024),
    )(right, left, mine, other, order, weight, features)


def per_device(features, weight, pre_act, grad_out, tile_ids, tile_count, tile_values):
    row = lax.axis_index("row")
    col = lax.axis_index("col")
    x, y = col % NX, col // NX
    z, core = row // 2, row % 2

    pre, grad = pre_act.T, grad_out.T
    masked = jnp.where(pre > 0, grad, jnp.zeros_like(grad))
    half = masked.shape[0] // 2
    along_x = jnp.concatenate(line(shift_x, masked[:half]), axis=0)
    along_y = jnp.concatenate(line(shift_y, masked[half:]), axis=0)

    place = jnp.arange(256, dtype=jnp.int32)
    second = place // 128
    outer, inner = place // 32 % 4, place // 8 % 4
    dy = jnp.where(second == 0, outer, inner)
    dx = jnp.where(second == 0, inner, outer)
    feature = ((y + dy) % NY * NX + (x + dx) % NX) * 16 + second * 8 + place % 8
    order = (place[:, None] == feature[None, :]).astype(BF)

    info = jnp.stack([z, core]).astype(jnp.int32)
    tile_ids, along_x, along_y = lax.optimization_barrier((tile_ids, along_x, along_y))
    table, values = list_pairs(tile_ids, tile_count, info, tile_values[0, 0])
    pieces = line_by_hops(shift_y, along_x) + line_by_hops(shift_x, along_y)

    right, left = [], []
    for stage in range(STAGES):
        mine, other = tile_products(stage, table, info, pieces, values)
        other = swap_core(other)
        right = [shift_z(add_bf(*right, mine[0], other[0]), 1)]
        if stage < STAGES - 1:
            left = [shift_z(add_bf(*left, mine[1], other[1]), -1)]

    grad_in, term = finish(right[0], left[0], mine, other, order, weight, features)
    parts = lax.all_to_all(term, ("row", "col"), 0, 0, tiled=True)
    grad_weight = jnp.sum(parts, axis=0).reshape(16, 16)
    return grad_in, grad_weight


def solution(mesh):
    return jax.shard_map(
        per_device,
        mesh=mesh,
        in_specs=(
            P(("col", "row"), None),
            P(),
            P("row", "col"),
            P("row", "col"),
            P("row", "col", None),
            P("row", "col"),
            P("row", "col", None, None, None),
        ),
        out_specs=(P(("col", "row"), None), P("row", "col")),
        check_vma=False,
    )
```

time: 579 us -> 128 us (0.22)
  waiting for transfers between devices: 367 us -> 26 us
  other arithmetic: 104 us -> 3.14 us
  local copies, waits for them, and re-layouts: 51.4 us -> 7.31 us
  matrix products: 41 us -> 0 us
  starting transfers between devices: 0.12 us -> 39.3 us
  blocking collectives: 0 us -> 31.6 us
  Pallas kernels: 0 us -> 18 us
  between operations: 13.8 us -> 1.46 us
    psum x1 -> x0, waiting for transfers between devices: 252 us -> none  [per_device(): whole_sum = lax.psum(weight_term, ('row', 'col'))]
    scatter-add x5 -> x0, other arithmetic: 98 us -> none  [add_block(): return running.at[block_list % col_tiles].add(product)]
    reduce_scatter x1 -> x0, waiting for transfers between devices: 67.3 us -> none  [per_device(): lax.psum_scatter(partial_value, 'row', scatter_dimension=0, tiled=True)]
    all_gather x1 -> x0, waiting for transfers between devices: 47.2 us -> none  [per_device(): gathered = lax.all_gather(grad_pre, 'col', axis=1, tiled=True)]
    dot_general x7 -> x0, matrix products: 41 us -> none  [the longest x5 37 us: add_block(): jnp.einsum('tkn,tkf->tnf', block_values, picked, preferred_element_type=j...]
    ppermute x0 -> x25, starting transfers between devices: none -> 39.3 us  [the longest x7 11.1 us: shift_x(): return lax.ppermute(array, 'col', pairs)]
    all_to_all x0 -> x1, blocking collectives: none -> 31.6 us  [per_device(): parts = lax.all_to_all(term, ('row', 'col'), 0, 0, tiled=True)]
    ppermute x0 -> x25, waiting for transfers between devices: none -> 26 us  [the longest x7 15.1 us: shift_z(): return lax.ppermute(array, 'row', pairs)]
  transfers between devices with their start and end apart: 3 -> 25, of which waited for: 3 -> 8; matrix products, arithmetic and copies ran while one was open for 3% -> 4% of each run, Pallas kernels for 0% -> 11%
where the time goes in v1:
time: 128 us; the launch traced here: 127 us
  starting transfers between devices  39.3 us (31%)
  blocking collectives  31.6 us (25%)
  waiting for transfers between devices  26 us (20%)
  Pallas kernels  18 us (14%)
  local copies, waits for them, and re-layouts  7.31 us (6%)
  other arithmetic  3.14 us (2%)
  between operations  1.46 us (1%)
    all_to_all x1, blocking collectives, per_device(): parts = lax.all_to_all(term, ('row', 'col'), 0, 0, tiled=True)  31.6 us
    ppermute x7, waiting for transfers between devices, shift_z(): return lax.ppermute(array, 'row', pairs)  15.1 us
    pallas_call x4, Pallas kernels, tile_products(): pl.pallas_call(functools.partial(tile_kernel, stage), in_specs=[smem] * 2...  11.8 us
    ppermute x7, starting transfers between devices, shift_x(): return lax.ppermute(array, 'col', pairs)  11.1 us
    ppermute x7, waiting for transfers between devices, shift_y(): return lax.ppermute(array, 'col', pairs)  10.8 us
    ppermute x7, starting transfers between devices, shift_y(): return lax.ppermute(array, 'col', pairs)  10.4 us
    ppermute x7, starting transfers between devices, shift_z(): return lax.ppermute(array, 'row', pairs)  9.1 us
    ppermute x4, starting transfers between devices, swap_core(): return lax.ppermute(array, 'row', [(i, i ^ 1) for i in range(2 * NZ)])  8.68 us
  transfers between devices with their start and end apart: 25, of which 8 were waited for; matrix products, arithmetic and copies ran while one was open for 4% of the time, Pallas kernels for 11%

profile of v1, /device:TPU:1, one launch (start us, length us, event | category | flops | bytes accessed | tf_op | source)
XLA Modules:
  0.0 126.7 jit_solution(2340063725145910483)
XLA Ops:
  0.6 1.1 fusion.5
  1.7 2.1 %collective-permute-start.2 = (bf16[8,8192]{1,0:T(8,128)(2,1)S(1)}, bf16[8,8192]{1,0:T(8,128)(2,1)S(1)}, u32[]{:S(2)}, u32[]{:S(2)}) collective-permute-start(bf16[8,8192]{1,0:T(8,128)(2,1)S(1)} %get-tuple-element.39), channel_id=1, source_target_pairs={{0,1},{1,2},{2,3},{3,0},{4,5},{5,6},{6,7},{7,4},{8,9},{9,10},{10,1... | collective-permute-start | bytes 393224 | tf_op jit(solution)/shard_map/ppermute | solution.py:25
  3.8 2.5 %collective-permute-start.1 = (bf16[8,8192]{1,0:T(8,128)(2,1)S(1)}, bf16[8,8192]{1,0:T(8,128)(2,1)S(1)}, u32[]{:S(2)}, u32[]{:S(2)}) collective-permute-start(bf16[8,8192]{1,0:T(8,128)(2,1)S(1)} %get-tuple-element.39), channel_id=1, source_target_pairs={{0,2},{1,3},{2,0},{3,1},{4,6},{5,7},{6,4},{7,5},{8,10},{9,11},{10,... | collective-permute-start | bytes 393224 | tf_op jit(solution)/shard_map/ppermute | solution.py:25
  6.3 1.2 collective-permute-start
  7.4 1.3 %collective-permute-start.5 = (bf16[8,8192]{1,0:T(8,128)(2,1)S(1)}, bf16[8,8192]{1,0:T(8,128)(2,1)S(1)}, u32[]{:S(2)}, u32[]{:S(2)}) collective-permute-start(bf16[8,8192]{1,0:T(8,128)(2,1)S(1)} %get-tuple-element.38), channel_id=1, source_target_pairs={{0,4},{1,5},{2,6},{3,7},{4,8},{5,9},{6,10},{7,11},{8,12},{9,13},{1... | collective-permute-start | bytes 393224 | tf_op jit(solution)/shard_map/ppermute | solution.py:30
  8.7 2.6 %collective-permute-start.4 = (bf16[8,8192]{1,0:T(8,128)(2,1)S(1)}, bf16[8,8192]{1,0:T(8,128)(2,1)S(1)}, u32[]{:S(2)}, u32[]{:S(2)}) collective-permute-start(bf16[8,8192]{1,0:T(8,128)(2,1)S(1)} %get-tuple-element.38), channel_id=1, source_target_pairs={{0,8},{1,9},{2,10},{3,11},{4,12},{5,13},{6,14},{7,15},{8,0},{9,1},... | collective-permute-start | bytes 393224 | tf_op jit(solution)/shard_map/ppermute | solution.py:30
  11.4 1.1 collective-permute-start.3
  12.8 3.1 %collective-permute-done.4 = bf16[8,8192]{1,0:T(8,128)(2,1)S(1)} collective-permute-done((bf16[8,8192]{1,0:T(8,128)(2,1)S(1)}, bf16[8,8192]{1,0:T(8,128)(2,1)S(1)}, u32[]{:S(2)}, u32[]{:S(2)}) %collective-permute-start.4) | collective-permute-done | bytes 131104 | tf_op jit(solution)/shard_map/ppermute | solution.py:30
  16.7 2.6 %collective-permute-start.6 = (bf16[32,8192]{1,0:T(8,128)(2,1)S(1)}, bf16[32,8192]{1,0:T(8,128)(2,1)S(1)}, u32[]{:S(2)}, u32[]{:S(2)}) collective-permute-start(bf16[32,8192]{1,0:T(8,128)(2,1)S(1)} %pad_maximum_fusion.refs_0_), channel_id=1, source_target_pairs={{0,12},{1,13},{2,14},{3,15},{4,0},{5,1},{6,2},{7,3},{8,4},{9,5},{1... | collective-permute-start | bytes 1572872 | tf_op jit(solution)/shard_map/ppermute | solution.py:30
  19.6 2.4 %collective-permute-start.10 = (bf16[32,8192]{1,0:T(8,128)(2,1)S(1)}, bf16[32,8192]{1,0:T(8,128)(2,1)S(1)}, u32[]{:S(2)}, u32[]{:S(2)}) collective-permute-start(bf16[32,8192]{1,0:T(8,128)(2,1)S(1)} %pad_maximum_fusion.1.refs_5_), channel_id=1, source_target_pairs={{0,3},{1,0},{2,1},{3,2},{4,7},{5,4},{6,5},{7,6},{8,11},{9,8},{10,9... | collective-permute-start | bytes 1572872 | tf_op jit(solution)/shard_map/ppermute | solution.py:25
  21.9 6.9 %collective-permute-done.7.refs_4_ = bf16[32,8192]{1,0:T(8,128)(2,1)S(1)} collective-permute-done((bf16[32,8192]{1,0:T(8,128)(2,1)S(1)}, bf16[32,8192]{1,0:T(8,128)(2,1)S(1)}, u32[]{:S(2)}, u32[]{:S(2)}) %collective-permute-start.7) | collective-permute-done | bytes 524320 | tf_op jit(solution)/shard_map/ppermute | solution.py:30
  30.2 2.7 %collective-permute-start.9 = (bf16[16,8192]{1,0:T(8,128)(2,1)}, bf16[16,8192]{1,0:T(8,128)(2,1)}, u32[]{:S(2)}, u32[]{:S(2)}) collective-permute-start(bf16[16,8192]{1,0:T(8,128)(2,1)} %slice.83), channel_id=1, source_target_pairs={{0,12},{1,13},{2,14},{3,15},{4,0},{5,1},{6,2},{7,3},{8,4},{9,5},{1... | collective-permute-start | bytes 786440 | tf_op jit(solution)/shard_map/ppermute | solution.py:30
  34.8 2.2 %collective-permute-start.13 = (bf16[16,8192]{1,0:T(8,128)(2,1)}, bf16[16,8192]{1,0:T(8,128)(2,1)}, u32[]{:S(2)}, u32[]{:S(2)}) collective-permute-start(bf16[16,8192]{1,0:T(8,128)(2,1)} %slice.85), channel_id=1, source_target_pairs={{0,3},{1,0},{2,1},{3,2},{4,7},{5,4},{6,5},{7,6},{8,11},{9,8},{10,9... | collective-permute-start | bytes 786440 | tf_op jit(solution)/shard_map/ppermute | solution.py:25
  38.4 4.5 %shard_map.86 = (s32[4,256]{1,0:T(4,128)S(1)}, bf16[320,128,128]{2,1,0:T(8,128)(2,1)S(1)}) custom-call(s32[1,320]{1,0:T(1,128)S(1)} %bitcast.52, s32[1,1]{1,0:T(1,128)S(6)} %copy.10.count_ref, s32[2]{0:T(128)S(1)} %pad_add_fusion.info_ref, bf16[320,128,128]{2,1,0:T(8,128)(2,1)} %bitcast.53), custom_call_target="tpu_custom_call" | custom-call | bytes 14000000 | tf_op jit(solution)/shard_map/pallas_call | solution.py:120
  43.0 2.7 %shard_map.87 = (bf16[2,256,512]{2,1,0:T(8,128)(2,1)S(1)}, bf16[2,256,512]{2,1,0:T(8,128)(2,1)S(1)}) custom-call(s32[4,256]{1,0:T(4,128)S(1)} %get-tuple-element.18.table_ref, s32[2]{0:T(128)S(1)} %pad_add_fusion.info_ref, bf16[32,8192]{1,0:T(8,128)(2,1)S(1)} %pad_maximum_fusion.refs_0_, bf16[32,8192]{1,0:T(8,128)(2,1)S(1)} %collective-permute-done.6.refs_1_, ...), custom_call_target="tpu_custom_call" | custom-call | bytes 1000000 | tf_op jit(solution)/shard_map/pallas_call | solution.py:188
  45.7 4.9 %collective-permute-start.14 = (bf16[2,256,512]{2,1,0:T(8,128)(2,1)S(1)}, bf16[2,256,512]{2,1,0:T(8,128)(2,1)S(1)}, u32[]{:S(2)}, u32[]{:S(2)}) collective-permute-start(bf16[2,256,512]{2,1,0:T(8,128)(2,1)S(1)} %get-tuple-element.23), channel_id=1, source_target_pairs={{0,16},{16,0},{32,48},{48,32},{64,80},{80,64},{96,112},{112,96},{1... | collective-permute-start | bytes 1572872 | tf_op jit(solution)/shard_map/ppermute | solution.py:39
  50.6 2.6 %shard_map.88 = (bf16[2,256,512]{2,1,0:T(8,128)(2,1)S(1)}, bf16[2,256,512]{2,1,0:T(8,128)(2,1)S(1)}) custom-call(s32[4,256]{1,0:T(4,128)S(1)} %get-tuple-element.18.table_ref, s32[2]{0:T(128)S(1)} %pad_add_fusion.info_ref, bf16[32,8192]{1,0:T(8,128)(2,1)S(1)} %pad_maximum_fusion.refs_0_, bf16[32,8192]{1,0:T(8,128)(2,1)S(1)} %collective-permute-done.6.refs_1_, ...), custom_call_target="tpu_custom_call" | custom-call | bytes 1000000 | tf_op jit(solution)/shard_map/pallas_call | solution.py:188
  53.2 1.0 collective-permute-start.16
  54.4 4.7 %collective-permute-start.22 = (bf16[256,512]{1,0:T(8,128)(2,1)S(1)}, bf16[256,512]{1,0:T(8,128)(2,1)S(1)}, u32[]{:S(2)}, u32[]{:S(2)}) collective-permute-start(bf16[256,512]{1,0:T(8,128)(2,1)S(1)} %get-tuple-element.36), channel_id=1, source_target_pairs={{0,224},{16,240},{32,0},{48,16},{64,32},{80,48},{96,64},{112,80},{... | collective-permute-start | bytes 786440 | tf_op jit(solution)/shard_map/ppermute | solution.py:35
  59.1 3.0 %shard_map.89 = (bf16[2,256,512]{2,1,0:T(8,128)(2,1)S(1)}, bf16[2,256,512]{2,1,0:T(8,128)(2,1)S(1)}) custom-call(s32[4,256]{1,0:T(4,128)S(1)} %get-tuple-element.18.table_ref, s32[2]{0:T(128)S(1)} %pad_add_fusion.info_ref, bf16[32,8192]{1,0:T(8,128)(2,1)S(1)} %pad_maximum_fusion.refs_0_, bf16[32,8192]{1,0:T(8,128)(2,1)S(1)} %collective-permute-done.6.refs_1_, ...), custom_call_target="tpu_custom_call" | custom-call | bytes 1000000 | tf_op jit(solution)/shard_map/pallas_call | solution.py:188
  62.7 1.6 %collective-permute-done.22 = bf16[256,512]{1,0:T(8,128)(2,1)S(1)} collective-permute-done((bf16[256,512]{1,0:T(8,128)(2,1)S(1)}, bf16[256,512]{1,0:T(8,128)(2,1)S(1)}, u32[]{:S(2)}, u32[]{:S(2)}) %collective-permute-start.22) | collective-permute-done | bytes 262176 | tf_op jit(solution)/shard_map/ppermute | solution.py:35
  64.3 3.1 %collective-permute-done.15 = bf16[256,512]{1,0:T(8,128)(2,1)S(1)} collective-permute-done((bf16[256,512]{1,0:T(8,128)(2,1)S(1)}, bf16[256,512]{1,0:T(8,128)(2,1)S(1)}, u32[]{:S(2)}, u32[]{:S(2)}) %collective-permute-start.15) | collective-permute-done | bytes 262176 | tf_op jit(solution)/shard_map/ppermute | solution.py:35
  68.0 1.1 collective-permute-start.17
  69.1 3.5 %shard_map.90 = (bf16[2,256,512]{2,1,0:T(8,128)(2,1)S(1)}, bf16[2,256,512]{2,1,0:T(8,128)(2,1)}) custom-call(s32[4,256]{1,0:T(4,128)S(1)} %get-tuple-element.18.table_ref, s32[2]{0:T(128)S(1)} %pad_add_fusion.info_ref, bf16[32,8192]{1,0:T(8,128)(2,1)S(1)} %pad_maximum_fusion.refs_0_, bf16[32,8192]{1,0:T(8,128)(2,1)S(1)} %collective-permute-done.6.refs_1_, ...), custom_call_target="tpu_custom_call" | custom-call | bytes 1000000 | tf_op jit(solution)/shard_map/pallas_call | solution.py:188
  73.4 2.2 %collective-permute-start.20 = (bf16[2,256,512]{2,1,0:T(8,128)(2,1)}, bf16[2,256,512]{2,1,0:T(8,128)(2,1)S(1)}, u32[]{:S(2)}, u32[]{:S(2)}) collective-permute-start(bf16[2,256,512]{2,1,0:T(8,128)(2,1)} %get-tuple-element.29), channel_id=1, source_target_pairs={{0,16},{16,0},{32,48},{48,32},{64,80},{80,64},{96,112},{112,96},{1... | collective-permute-start | bytes 1572872 | tf_op jit(solution)/shard_map/ppermute | solution.py:39
  76.3 2.3 %collective-permute-start.24 = (bf16[256,512]{1,0:T(8,128)(2,1)S(1)}, bf16[256,512]{1,0:T(8,128)(2,1)S(1)}, u32[]{:S(2)}, u32[]{:S(2)}) collective-permute-start(bf16[256,512]{1,0:T(8,128)(2,1)S(1)} %get-tuple-element.32), channel_id=1, source_target_pairs={{0,224},{16,240},{32,0},{48,16},{64,32},{80,48},{96,64},{112,80},{... | collective-permute-start | bytes 786440 | tf_op jit(solution)/shard_map/ppermute | solution.py:35
  78.6 4.1 %collective-permute-done.19 = bf16[256,512]{1,0:T(8,128)(2,1)S(1)} collective-permute-done((bf16[256,512]{1,0:T(8,128)(2,1)S(1)}, bf16[256,512]{1,0:T(8,128)(2,1)S(1)}, u32[]{:S(2)}, u32[]{:S(2)}) %collective-permute-start.19) | collective-permute-done | bytes 262176 | tf_op jit(solution)/shard_map/ppermute | solution.py:35
  82.7 1.1 fusion.2
  83.9 6.4 %collective-permute-done.21.right_ref = bf16[256,512]{1,0:T(8,128)(2,1)S(1)} collective-permute-done((bf16[256,512]{1,0:T(8,128)(2,1)S(1)}, bf16[256,512]{1,0:T(8,128)(2,1)S(1)}, u32[]{:S(2)}, u32[]{:S(2)}) %collective-permute-start.21) | collective-permute-done | bytes 262176 | tf_op jit(solution)/shard_map/ppermute | solution.py:35
  90.3 1.0 copy-done.1
  92.3 1.6 %shard_map.91 = (bf16[512,256]{1,0:T(8,128)(2,1)}, f32[256,256]{1,0:T(8,128)S(1)}) custom-call(bf16[256,512]{1,0:T(8,128)(2,1)S(1)} %collective-permute-done.21.right_ref, bf16[256,512]{1,0:T(8,128)(2,1)S(1)} %collective-permute-done.24.left_ref, bf16[2,256,512]{2,1,0:T(8,128)(2,1)S(1)} %copy-done.1, ...), custom_call_target="tpu_custom_call" | custom-call | tf_op jit(solution)/shard_map/pallas_call | solution.py:236
  94.2 31.6 %all_to_all.9 = f32[256,1,256]{2,1,0:T(1,128)S(1)} all-to-all(f32[256,1,256]{2,1,0:T(1,128)S(1)} %copy.9), channel_id=1, replica_groups=mesh['row'=16,'col'=16] {'row','col'}, dimensions={0} | all-to-all | bytes 524288 | tf_op jit(solution)/shard_map/all_to_all | solution.py:280
  (53 shorter events, 10.7 us)
Async XLA Ops:
  1.7 9.6 %collective-permute-start.2 = (bf16[8,8192]{1,0:T(8,128)(2,1)S(1)}, bf16[8,8192]{1,0:T(8,128)(2,1)S(1)}, u32[]{:S(2)}, u32[]{:S(2)}) collective-permute-start(bf16[8,8192]{1,0:T(8,128)(2,1)S(1)} %get-tuple-element.39), channel_id=1, source_target_pairs={{0,1},{1,2},{2,3},{3,0},{4,5},{5,6},{6,7},{7,4},{8,9},{9,10},{10,1... | collective-permute-start | bytes 393224 | tf_op jit(solution)/shard_map/ppermute | solution.py:25
  3.8 8.6 %collective-permute-start.1 = (bf16[8,8192]{1,0:T(8,128)(2,1)S(1)}, bf16[8,8192]{1,0:T(8,128)(2,1)S(1)}, u32[]{:S(2)}, u32[]{:S(2)}) collective-permute-start(bf16[8,8192]{1,0:T(8,128)(2,1)S(1)} %get-tuple-element.39), channel_id=1, source_target_pairs={{0,2},{1,3},{2,0},{3,1},{4,6},{5,7},{6,4},{7,5},{8,10},{9,11},{10,... | collective-permute-start | bytes 393224 | tf_op jit(solution)/shard_map/ppermute | solution.py:25
  6.3 6.2 %collective-permute-start = (bf16[8,8192]{1,0:T(8,128)(2,1)S(1)}, bf16[8,8192]{1,0:T(8,128)(2,1)S(1)}, u32[]{:S(2)}, u32[]{:S(2)}) collective-permute-start(bf16[8,8192]{1,0:T(8,128)(2,1)S(1)} %get-tuple-element.39), channel_id=1, source_target_pairs={{0,3},{1,0},{2,1},{3,2},{4,7},{5,4},{6,5},{7,6},{8,11},{9,8},{10,9... | collective-permute-start | bytes 393224 | tf_op jit(solution)/shard_map/ppermute | solution.py:25
  7.4 5.4 %collective-permute-start.5 = (bf16[8,8192]{1,0:T(8,128)(2,1)S(1)}, bf16[8,8192]{1,0:T(8,128)(2,1)S(1)}, u32[]{:S(2)}, u32[]{:S(2)}) collective-permute-start(bf16[8,8192]{1,0:T(8,128)(2,1)S(1)} %get-tuple-element.38), channel_id=1, source_target_pairs={{0,4},{1,5},{2,6},{3,7},{4,8},{5,9},{6,10},{7,11},{8,12},{9,13},{1... | collective-permute-start | bytes 393224 | tf_op jit(solution)/shard_map/ppermute | solution.py:30
  8.7 7.1 %collective-permute-start.4 = (bf16[8,8192]{1,0:T(8,128)(2,1)S(1)}, bf16[8,8192]{1,0:T(8,128)(2,1)S(1)}, u32[]{:S(2)}, u32[]{:S(2)}) collective-permute-start(bf16[8,8192]{1,0:T(8,128)(2,1)S(1)} %get-tuple-element.38), channel_id=1, source_target_pairs={{0,8},{1,9},{2,10},{3,11},{4,12},{5,13},{6,14},{7,15},{8,0},{9,1},... | collective-permute-start | bytes 393224 | tf_op jit(solution)/shard_map/ppermute | solution.py:30
  11.4 5.1 %collective-permute-start.3 = (bf16[8,8192]{1,0:T(8,128)(2,1)S(1)}, bf16[8,8192]{1,0:T(8,128)(2,1)S(1)}, u32[]{:S(2)}, u32[]{:S(2)}) collective-permute-start(bf16[8,8192]{1,0:T(8,128)(2,1)S(1)} %get-tuple-element.38), channel_id=1, source_target_pairs={{0,12},{1,13},{2,14},{3,15},{4,0},{5,1},{6,2},{7,3},{8,4},{9,5},{1... | collective-permute-start | bytes 393224 | tf_op jit(solution)/shard_map/ppermute | solution.py:30
  16.5 12.3 %collective-permute-start.7 = (bf16[32,8192]{1,0:T(8,128)(2,1)S(1)}, bf16[32,8192]{1,0:T(8,128)(2,1)S(1)}, u32[]{:S(2)}, u32[]{:S(2)}) collective-permute-start(bf16[32,8192]{1,0:T(8,128)(2,1)S(1)} %pad_maximum_fusion.refs_0_), channel_id=1, source_target_pairs={{0,4},{1,5},{2,6},{3,7},{4,8},{5,9},{6,10},{7,11},{8,12},{9,13},{1... | collective-permute-start | bytes 1572872 | tf_op jit(solution)/shard_map/ppermute | solution.py:30
  16.7 12.9 %collective-permute-start.6 = (bf16[32,8192]{1,0:T(8,128)(2,1)S(1)}, bf16[32,8192]{1,0:T(8,128)(2,1)S(1)}, u32[]{:S(2)}, u32[]{:S(2)}) collective-permute-start(bf16[32,8192]{1,0:T(8,128)(2,1)S(1)} %pad_maximum_fusion.refs_0_), channel_id=1, source_target_pairs={{0,12},{1,13},{2,14},{3,15},{4,0},{5,1},{6,2},{7,3},{8,4},{9,5},{1... | collective-permute-start | bytes 1572872 | tf_op jit(solution)/shard_map/ppermute | solution.py:30
  19.3 13.6 %collective-permute-start.11 = (bf16[32,8192]{1,0:T(8,128)(2,1)S(1)}, bf16[32,8192]{1,0:T(8,128)(2,1)S(1)}, u32[]{:S(2)}, u32[]{:S(2)}) collective-permute-start(bf16[32,8192]{1,0:T(8,128)(2,1)S(1)} %pad_maximum_fusion.1.refs_5_), channel_id=1, source_target_pairs={{0,1},{1,2},{2,3},{3,0},{4,5},{5,6},{6,7},{7,4},{8,9},{9,10},{10,1... | collective-permute-start | bytes 1572872 | tf_op jit(solution)/shard_map/ppermute | solution.py:25
  19.6 14.6 %collective-permute-start.10 = (bf16[32,8192]{1,0:T(8,128)(2,1)S(1)}, bf16[32,8192]{1,0:T(8,128)(2,1)S(1)}, u32[]{:S(2)}, u32[]{:S(2)}) collective-permute-start(bf16[32,8192]{1,0:T(8,128)(2,1)S(1)} %pad_maximum_fusion.1.refs_5_), channel_id=1, source_target_pairs={{0,3},{1,0},{2,1},{3,2},{4,7},{5,4},{6,5},{7,6},{8,11},{9,8},{10,9... | collective-permute-start | bytes 1572872 | tf_op jit(solution)/shard_map/ppermute | solution.py:25
  29.5 13.5 %collective-permute-start.8 = (bf16[16,8192]{1,0:T(8,128)(2,1)}, bf16[16,8192]{1,0:T(8,128)(2,1)S(1)}, u32[]{:S(2)}, u32[]{:S(2)}) collective-permute-start(bf16[16,8192]{1,0:T(8,128)(2,1)} %slice.82), channel_id=1, source_target_pairs={{0,4},{1,5},{2,6},{3,7},{4,8},{5,9},{6,10},{7,11},{8,12},{9,13},{1... | collective-permute-start | bytes 786440 | tf_op jit(solution)/shard_map/ppermute | solution.py:30
  30.2 12.8 %collective-permute-start.9 = (bf16[16,8192]{1,0:T(8,128)(2,1)}, bf16[16,8192]{1,0:T(8,128)(2,1)}, u32[]{:S(2)}, u32[]{:S(2)}) collective-permute-start(bf16[16,8192]{1,0:T(8,128)(2,1)} %slice.83), channel_id=1, source_target_pairs={{0,12},{1,13},{2,14},{3,15},{4,0},{5,1},{6,2},{7,3},{8,4},{9,5},{1... | collective-permute-start | bytes 786440 | tf_op jit(solution)/shard_map/ppermute | solution.py:30
  33.6 9.4 %collective-permute-start.12 = (bf16[16,8192]{1,0:T(8,128)(2,1)}, bf16[16,8192]{1,0:T(8,128)(2,1)}, u32[]{:S(2)}, u32[]{:S(2)}) collective-permute-start(bf16[16,8192]{1,0:T(8,128)(2,1)} %slice.84), channel_id=1, source_target_pairs={{0,1},{1,2},{2,3},{3,0},{4,5},{5,6},{6,7},{7,4},{8,9},{9,10},{10,1... | collective-permute-start | bytes 786440 | tf_op jit(solution)/shard_map/ppermute | solution.py:25
  34.8 8.2 %collective-permute-start.13 = (bf16[16,8192]{1,0:T(8,128)(2,1)}, bf16[16,8192]{1,0:T(8,128)(2,1)}, u32[]{:S(2)}, u32[]{:S(2)}) collective-permute-start(bf16[16,8192]{1,0:T(8,128)(2,1)} %slice.85), channel_id=1, source_target_pairs={{0,3},{1,0},{2,1},{3,2},{4,7},{5,4},{6,5},{7,6},{8,11},{9,8},{10,9... | collective-permute-start | bytes 786440 | tf_op jit(solution)/shard_map/ppermute | solution.py:25
  37.7 0.7 copy-start.4
  45.7 8.5 %collective-permute-start.14 = (bf16[2,256,512]{2,1,0:T(8,128)(2,1)S(1)}, bf16[2,256,512]{2,1,0:T(8,128)(2,1)S(1)}, u32[]{:S(2)}, u32[]{:S(2)}) collective-permute-start(bf16[2,256,512]{2,1,0:T(8,128)(2,1)S(1)} %get-tuple-element.23), channel_id=1, source_target_pairs={{0,16},{16,0},{32,48},{48,32},{64,80},{80,64},{96,112},{112,96},{1... | collective-permute-start | bytes 1572872 | tf_op jit(solution)/shard_map/ppermute | solution.py:39
  53.2 9.5 %collective-permute-start.16 = (bf16[2,256,512]{2,1,0:T(8,128)(2,1)S(1)}, bf16[2,256,512]{2,1,0:T(8,128)(2,1)S(1)}, u32[]{:S(2)}, u32[]{:S(2)}) collective-permute-start(bf16[2,256,512]{2,1,0:T(8,128)(2,1)S(1)} %get-tuple-element.25), channel_id=1, source_target_pairs={{0,16},{16,0},{32,48},{48,32},{64,80},{80,64},{96,112},{112,96},{1... | collective-permute-start | bytes 1572872 | tf_op jit(solution)/shard_map/ppermute | solution.py:39
  54.4 9.9 %collective-permute-start.22 = (bf16[256,512]{1,0:T(8,128)(2,1)S(1)}, bf16[256,512]{1,0:T(8,128)(2,1)S(1)}, u32[]{:S(2)}, u32[]{:S(2)}) collective-permute-start(bf16[256,512]{1,0:T(8,128)(2,1)S(1)} %get-tuple-element.36), channel_id=1, source_target_pairs={{0,224},{16,240},{32,0},{48,16},{64,32},{80,48},{96,64},{112,80},{... | collective-permute-start | bytes 786440 | tf_op jit(solution)/shard_map/ppermute | solution.py:35
  59.1 8.3 %collective-permute-start.15 = (bf16[256,512]{1,0:T(8,128)(2,1)S(1)}, bf16[256,512]{1,0:T(8,128)(2,1)S(1)}, u32[]{:S(2)}, u32[]{:S(2)}) collective-permute-start(bf16[256,512]{1,0:T(8,128)(2,1)S(1)} %get-tuple-element.37), channel_id=1, source_target_pairs={{0,32},{16,48},{32,64},{48,80},{64,96},{80,112},{96,128},{112,144}... | collective-permute-start | bytes 786440 | tf_op jit(solution)/shard_map/ppermute | solution.py:35
  62.1 28.1 %copy-start.3 = (bf16[256,256]{1,0:T(8,128)(2,1)S(1)}, bf16[256,256]{1,0:T(8,128)(2,1)}, u32[]{:S(2)}) copy-start(bf16[256,256]{1,0:T(8,128)(2,1)} %weight_ref.1) | copy-start | bytes 393220
  62.1 13.5 %collective-permute-start.18 = (bf16[2,256,512]{2,1,0:T(8,128)(2,1)S(1)}, bf16[2,256,512]{2,1,0:T(8,128)(2,1)S(1)}, u32[]{:S(2)}, u32[]{:S(2)}) collective-permute-start(bf16[2,256,512]{2,1,0:T(8,128)(2,1)S(1)} %get-tuple-element.27), channel_id=1, source_target_pairs={{0,16},{16,0},{32,48},{48,32},{64,80},{80,64},{96,112},{112,96},{1... | collective-permute-start | bytes 1572872 | tf_op jit(solution)/shard_map/ppermute | solution.py:39
  67.6 8.1 %collective-permute-start.23 = (bf16[256,512]{1,0:T(8,128)(2,1)S(1)}, bf16[256,512]{1,0:T(8,128)(2,1)S(1)}, u32[]{:S(2)}, u32[]{:S(2)}) collective-permute-start(bf16[256,512]{1,0:T(8,128)(2,1)S(1)} %get-tuple-element.34), channel_id=1, source_target_pairs={{0,224},{16,240},{32,0},{48,16},{64,32},{80,48},{96,64},{112,80},{... | collective-permute-start | bytes 786440 | tf_op jit(solution)/shard_map/ppermute | solution.py:35
  68.0 7.7 %collective-permute-start.17 = (bf16[256,512]{1,0:T(8,128)(2,1)S(1)}, bf16[256,512]{1,0:T(8,128)(2,1)S(1)}, u32[]{:S(2)}, u32[]{:S(2)}) collective-permute-start(bf16[256,512]{1,0:T(8,128)(2,1)S(1)} %get-tuple-element.35), channel_id=1, source_target_pairs={{0,32},{16,48},{32,64},{48,80},{64,96},{80,112},{96,128},{112,144}... | collective-permute-start | bytes 786440 | tf_op jit(solution)/shard_map/ppermute | solution.py:35
  72.6 0.8 copy-start
  73.4 5.2 %collective-permute-start.20 = (bf16[2,256,512]{2,1,0:T(8,128)(2,1)}, bf16[2,256,512]{2,1,0:T(8,128)(2,1)S(1)}, u32[]{:S(2)}, u32[]{:S(2)}) collective-permute-start(bf16[2,256,512]{2,1,0:T(8,128)(2,1)} %get-tuple-element.29), channel_id=1, source_target_pairs={{0,16},{16,0},{32,48},{48,32},{64,80},{80,64},{96,112},{112,96},{1... | collective-permute-start | bytes 1572872 | tf_op jit(solution)/shard_map/ppermute | solution.py:39
  75.9 6.8 %collective-permute-start.19 = (bf16[256,512]{1,0:T(8,128)(2,1)S(1)}, bf16[256,512]{1,0:T(8,128)(2,1)S(1)}, u32[]{:S(2)}, u32[]{:S(2)}) collective-permute-start(bf16[256,512]{1,0:T(8,128)(2,1)S(1)} %get-tuple-element.33), channel_id=1, source_target_pairs={{0,32},{16,48},{32,64},{48,80},{64,96},{80,112},{96,128},{112,144}... | collective-permute-start | bytes 786440 | tf_op jit(solution)/shard_map/ppermute | solution.py:35
  76.3 7.6 %collective-permute-start.24 = (bf16[256,512]{1,0:T(8,128)(2,1)S(1)}, bf16[256,512]{1,0:T(8,128)(2,1)S(1)}, u32[]{:S(2)}, u32[]{:S(2)}) collective-permute-start(bf16[256,512]{1,0:T(8,128)(2,1)S(1)} %get-tuple-element.32), channel_id=1, source_target_pairs={{0,224},{16,240},{32,0},{48,16},{64,32},{80,48},{96,64},{112,80},{... | collective-permute-start | bytes 786440 | tf_op jit(solution)/shard_map/ppermute | solution.py:35
  83.8 6.5 %collective-permute-start.21 = (bf16[256,512]{1,0:T(8,128)(2,1)S(1)}, bf16[256,512]{1,0:T(8,128)(2,1)S(1)}, u32[]{:S(2)}, u32[]{:S(2)}) collective-permute-start(bf16[256,512]{1,0:T(8,128)(2,1)S(1)} %fusion.2), channel_id=1, source_target_pairs={{0,32},{16,48},{32,64},{48,80},{64,96},{80,112},{96,128},{112,144}... | collective-permute-start | bytes 786440 | tf_op jit(solution)/shard_map/ppermute | solution.py:35
  90.3 1.0 copy-start.1
  91.3 0.9 copy-start.2

commit v2 on v1

--- a/solution.py
+++ b/solution.py
@@ -17,7 +17,7 @@
 STAGES = 4
 STAGE_COLS = COLS // STAGES
 GROUP = 4
-VMEM_LIMIT = 24 * 1024 * 1024
+VMEM_LIMIT = 20 * 1024 * 1024
 
 
 def shift_x(array, step):
@@ -49,7 +49,7 @@
     return block, shift(block, -1), shift(block, 2), shift(block, 1)
 
 
-def pair_kernel(ids_ref, count_ref, info_ref, values_hbm, table_ref, values_ref, value_sem):
+def pair_kernel(ids_ref, count_ref, values_hbm, table_ref, order_ref, values_ref, value_sem):
     copy = pltpu.make_async_copy(values_hbm, values_ref, value_sem)
     copy.start()
     slots = ids_ref.shape[1]
@@ -59,7 +59,7 @@
     live = slot < count_ref[0, 0]
     j = ids & (COLS - 1)
     i = lax.shift_right_logical(ids, 6) & (COLS - 1)
-    ahead = (lax.shift_right_logical(j, 3) - info_ref[0]) & (NZ - 1)
+    ahead = (lax.shift_right_logical(j, 3) - lax.axis_index("row") // 2) & (NZ - 1)
     is_right = (ahead >= 1) & (ahead <= 4)
     stage = jnp.where(is_right, 4 - ahead, 3 - ((NZ - ahead) & (NZ - 1)))
     rank = stage * STAGE_COLS + jnp.where(is_right, 0, 8) + (j & 7)
@@ -110,19 +110,30 @@
     table_ref[3:4, :COLS] = start.T[0:1].astype(jnp.int32)
     total = jnp.sum(pairs, axis=0, keepdims=True).astype(jnp.int32)
     table_ref[3:4, TILE : 2 * TILE] = jnp.broadcast_to(total, (1, TILE))
+
+    col = lax.axis_index("col")
+    place = lax.broadcasted_iota(jnp.int32, order_ref.shape, 1)
+    second = lax.shift_right_logical(place, 7)
+    outer, inner = lax.shift_right_logical(place, 5) & 3, lax.shift_right_logical(place, 3) & 3
+    dy = jnp.where(second == 0, outer, inner)
+    dx = jnp.where(second == 0, inner, outer)
+    device = ((col // NX + dy) & (NY - 1)) * NX + ((col % NX + dx) & (NX - 1))
+    feature = device * 16 + second * 8 + (place & 7)
+    order_ref[...] = flag(lax.broadcasted_iota(jnp.int32, order_ref.shape, 0) == feature)
     copy.wait()
 
 
-def list_pairs(tile_ids, tile_count, info, values):
+def list_pairs(tile_ids, tile_count, values):
     smem = pl.BlockSpec(memory_space=pltpu.SMEM)
     vmem = pl.BlockSpec(memory_space=pltpu.VMEM)
     room = 256
     return pl.pallas_call(
         pair_kernel,
-        in_specs=[vmem, smem, smem, pl.BlockSpec(memory_space=pl.ANY)],
-        out_specs=[vmem, vmem],
+        in_specs=[vmem, smem, pl.BlockSpec(memory_space=pl.ANY)],
+        out_specs=[vmem] * 3,
         out_shape=[
             jax.ShapeDtypeStruct((4, room), jnp.int32),
+            jax.ShapeDtypeStruct((256, 256), BF),
             jax.ShapeDtypeStruct(values.shape, BF),
         ],
         scratch_shapes=[pltpu.SemaphoreType.DMA],
@@ -131,14 +142,13 @@
     )(
         tile_ids.reshape(1, -1),
         tile_count,
-        info,
         pltpu.with_memory_space_constraint(values, pltpu.HBM),
     )
 
 
-def tile_kernel(stage, table_ref, info_ref, *refs):
+def tile_kernel(stage, table_ref, *refs):
     *pieces, values_ref, mine_ref, other_ref, acc_ref = refs
-    core = info_ref[1]
+    core = lax.axis_index("row") % 2
     width = acc_ref.shape[1]
     begin = table_ref[3, stage * STAGE_COLS]
     end = table_ref[3, (stage + 1) * STAGE_COLS if stage < STAGES - 1 else TILE]
@@ -181,28 +191,26 @@
             other_ref[side, :, lanes] = acc_ref[side * 8 + (1 - core) * 4 + q].astype(BF)
 
 
-def tile_products(stage, table, info, pieces, values):
+def tile_products(stage, table, pieces, values):
     width = sum(piece.shape[0] for piece in pieces)
     smem = pl.BlockSpec(memory_space=pltpu.SMEM)
     vmem = pl.BlockSpec(memory_space=pltpu.VMEM)
     return pl.pallas_call(
         functools.partial(tile_kernel, stage),
-        in_specs=[smem] * 2 + [vmem] * (len(pieces) + 1),
+        in_specs=[smem] + [vmem] * (len(pieces) + 1),
         out_specs=[vmem] * 2,
         scratch_shapes=[pltpu.VMEM((STAGE_COLS + 1, width, TILE), F32)],
         out_shape=[jax.ShapeDtypeStruct((2, width, 512), BF)] * 2,
         compiler_params=pltpu.CompilerParams(vmem_limit_bytes=VMEM_LIMIT),
         cost_estimate=pl.CostEstimate(flops=0, bytes_accessed=1_000_000, transcendentals=0),
-    )(table, info, *pieces, values)
+    )(table, *pieces, values)
 
 
 def add_bf(*terms):
     return sum(term.astype(F32) for term in terms).astype(BF)
 
 
-def final_kernel(
-    right_ref, left_ref, mine_ref, other_ref, order_ref, weight_ref, feat_ref, grad_ref, term_ref
-):
+def spread_kernel(right_ref, left_ref, mine_ref, other_ref, order_ref, weight_ref, grad_ref):
     held = right_ref[...].astype(F32) + left_ref[...].astype(F32)
     held = held + mine_ref[1].astype(F32) + other_ref[1].astype(F32)
     spread = lax.dot_general(
@@ -211,9 +219,36 @@
     grad_ref[...] = lax.dot_general(
         spread, weight_ref[...], (((0,), (1,)), ((), ())), preferred_element_type=F32
     ).astype(BF)
-    term = lax.dot_general(
-        feat_ref[...], spread, (((0,), (1,)), ((), ())), preferred_element_type=F32
-    )
+
+
+def finish(right, left, mine, other, order, weight):
+    return pl.pallas_call(
+        spread_kernel,
+        out_shape=jax.ShapeDtypeStruct((right.shape[1], weight.shape[0]), BF),
+        compiler_params=pltpu.CompilerParams(vmem_limit_bytes=8 * 1024 * 1024),
+        cost_estimate=pl.CostEstimate(flops=0, bytes_accessed=1_000_000, transcendentals=0),
+    )(right, left, mine, other, order, weight)
+
+
+def term_kernel(
+    sent_ref,
+    left_ref,
+    mine_ref,
+    other_ref,
+    order_ref,
+    ahead_ref,
+    feat_ref,
+    keep_ref,
+    give_ref,
+    laid_ref,
+):
+    held = left_ref[...].astype(F32) + mine_ref[1].astype(F32) + other_ref[1].astype(F32)
+    both = jnp.concatenate([held.astype(BF), sent_ref[...]], axis=1)
+    spread = lax.dot_general(
+        order_ref[...], both, (((1,), (0,)), ((), ())), preferred_element_type=F32
+    ).astype(BF)
+    nodes = jnp.concatenate([feat_ref[...], ahead_ref[...]], axis=0)
+    term = lax.dot_general(nodes, spread, (((0,), (1,)), ((), ())), preferred_element_type=F32)
     rows = lax.broadcasted_iota(jnp.int32, (8, TILE), 0)
     spans = lax.broadcasted_iota(jnp.int32, (8, TILE), 1) // 16
     for half in range(2):
@@ -227,57 +262,60 @@
             moved = jnp.where(keep[None], turned, moved)
         for r in range(16):
             for upper in range(2):
-                term_ref[
-                    r * 16 + half * 8 : r * 16 + half * 8 + 8, upper * TILE : (upper + 1) * TILE
+                laid_ref[
+                    r % 2,
+                    r // 2 * 16 + half * 8 : r // 2 * 16 + half * 8 + 8,
+                    upper * TILE : (upper + 1) * TILE,
                 ] = moved[2 * r + upper]
-
-
-def finish(right, left, mine, other, order, weight, features):
+    core = lax.axis_index("row") % 2
+    keep_ref[...] = laid_ref[core]
+    give_ref[...] = laid_ref[1 - core]
+
+
+def weight_term(sent, left, mine, other, order, ahead, features):
+    vmem = pl.BlockSpec(memory_space=pltpu.VMEM)
     return pl.pallas_call(
-        final_kernel,
-        out_shape=[
-            jax.ShapeDtypeStruct(features.shape, BF),
-            jax.ShapeDtypeStruct((256, 256), F32),
-        ],
-        compiler_params=pltpu.CompilerParams(vmem_limit_bytes=16 * 1024 * 1024),
-    )(right, left, mine, other, order, weight, features)
+        term_kernel,
+        in_specs=[vmem] * 7,
+        out_specs=[vmem] * 2,
+        out_shape=[jax.ShapeDtypeStruct((TILE, 256), F32)] * 2,
+        scratch_shapes=[pltpu.VMEM((2, TILE, 256), F32)],
+        compiler_params=pltpu.CompilerParams(vmem_limit_bytes=8 * 1024 * 1024),
+        cost_estimate=pl.CostEstimate(flops=0, bytes_accessed=1_000_000, transcendentals=0),
+    )(sent, left, mine, other, order, ahead, features)
 
 
 def per_device(features, weight, pre_act, grad_out, tile_ids, tile_count, tile_values):
-    row = lax.axis_index("row")
-    col = lax.axis_index("col")
-    x, y = col % NX, col // NX
-    z, core = row // 2, row % 2
-
     pre, grad = pre_act.T, grad_out.T
     masked = jnp.where(pre > 0, grad, jnp.zeros_like(grad))
     half = masked.shape[0] // 2
     along_x = jnp.concatenate(line(shift_x, masked[:half]), axis=0)
     along_y = jnp.concatenate(line(shift_y, masked[half:]), axis=0)
 
-    place = jnp.arange(256, dtype=jnp.int32)
-    second = place // 128
-    outer, inner = place // 32 % 4, place // 8 % 4
-    dy = jnp.where(second == 0, outer, inner)
-    dx = jnp.where(second == 0, inner, outer)
-    feature = ((y + dy) % NY * NX + (x + dx) % NX) * 16 + second * 8 + place % 8
-    order = (place[:, None] == feature[None, :]).astype(BF)
-
-    info = jnp.stack([z, core]).astype(jnp.int32)
-    tile_ids, along_x, along_y = lax.optimization_barrier((tile_ids, along_x, along_y))
-    table, values = list_pairs(tile_ids, tile_count, info, tile_values[0, 0])
+    tile_ids, along_x, along_y, nodes = lax.optimization_barrier(
+        (tile_ids, along_x, along_y, features)
+    )
+    ahead = shift_z(nodes, -1)
+    table, order, values = list_pairs(tile_ids, tile_count, tile_values[0, 0])
     pieces = line_by_hops(shift_y, along_x) + line_by_hops(shift_x, along_y)
 
+    table, ahead = lax.optimization_barrier((table, ahead))
     right, left = [], []
-    for stage in range(STAGES):
-        mine, other = tile_products(stage, table, info, pieces, values)
+    mine, other = tile_products(0, table, pieces, values)
+    for stage in range(STAGES - 1):
         other = swap_core(other)
-        right = [shift_z(add_bf(*right, mine[0], other[0]), 1)]
-        if stage < STAGES - 1:
-            left = [shift_z(add_bf(*left, mine[1], other[1]), -1)]
-
-    grad_in, term = finish(right[0], left[0], mine, other, order, weight, features)
-    parts = lax.all_to_all(term, ("row", "col"), 0, 0, tiled=True)
+        right = add_bf(*right, mine[0], other[0])
+        left = add_bf(*left, mine[1], other[1])
+        right, left = [shift_z(right, 1)], [shift_z(left, -1)]
+        mine, other = tile_products(stage + 1, table, pieces, values)
+    other = swap_core(other)
+    sent = add_bf(*right, mine[0], other[0])
+    keep, give = weight_term(sent, left[0], mine, other, order, ahead, features)
+    blocks = keep + swap_core(give)
+    right = shift_z(sent, 1)
+    groups = [[i for i in range(256) if i // 16 % 2 == c] for c in range(2)]
+    parts = lax.all_to_all(blocks, ("row", "col"), 0, 0, tiled=True, axis_index_groups=groups)
+    grad_in = finish(right, left[0], mine, other, order, weight)
     grad_weight = jnp.sum(parts, axis=0).reshape(16, 16)
     return grad_in, grad_weight
 

time: 128 us -> 110 us (0.86); the launches traced: 127 us -> 111 us
  blocking collectives: 31.6 us -> 0 us
  starting transfers between devices: 39.3 us -> 60.3 us
  local copies, waits for them, and re-layouts: 7.31 us -> 2.23 us
  waiting for transfers between devices: 26 us -> 29.7 us
  Pallas kernels: 18 us -> 15 us
    all_to_all x1 -> x0, blocking collectives: 31.6 us -> none  [per_device(): parts = lax.all_to_all(term, ('row', 'col'), 0, 0, tiled=True)]
    ppermute x7 -> x8, starting transfers between devices: 9.1 us -> 20.6 us  [shift_z(): return lax.ppermute(array, 'row', pairs)]
    all_to_all x0 -> x1, waiting for transfers between devices: none -> 9.83 us  [per_device(): lax.all_to_all(blocks, ('row', 'col'), 0, 0, tiled=True, axis_index_group...]
    all_to_all x0 -> x1, starting transfers between devices: none -> 8.52 us  [per_device(): lax.all_to_all(blocks, ('row', 'col'), 0, 0, tiled=True, axis_index_group...]
    ppermute x7, waiting for transfers between devices: 10.8 us -> 5.27 us  [shift_y(): return lax.ppermute(array, 'col', pairs)]
    pallas_call x6 -> x7, Pallas kernels: 18 us -> 15 us  [the longest x4 8.51 us: tile_products(): pl.pallas_call(functools.partial(tile_kernel, stage), in_specs=[smem] + [...]
    unnamed x10 -> x6, local copies, waits for them, and re-layouts: 3.48 us -> 0.69 us
    ppermute x7 -> x8, waiting for transfers between devices: 15.1 us -> 13.6 us  [shift_z(): return lax.ppermute(array, 'row', pairs)]
  transfers between devices with their start and end apart: 25 -> 28, of which waited for: 8 -> 11; matrix products, arithmetic and copies ran while one was open for 4% -> 1% of each run, Pallas kernels for 11% -> 11%
where the time goes in v2:
time: 110 us; the launch traced here: 111 us
  starting transfers between devices  60.3 us (55%)
  waiting for transfers between devices  29.7 us (27%)
  Pallas kernels  15 us (14%)
  local copies, waits for them, and re-layouts  2.23 us (2%)
  other arithmetic  1.96 us (2%)
  between operations  1.54 us (1%)
    ppermute x8, starting transfers between devices, shift_z(): return lax.ppermute(array, 'row', pairs)  20.6 us
    ppermute x8, waiting for transfers between devices, shift_z(): return lax.ppermute(array, 'row', pairs)  13.6 us
    ppermute x7, starting transfers between devices, shift_x(): return lax.ppermute(array, 'col', pairs)  11.2 us
    ppermute x7, starting transfers between devices, shift_y(): return lax.ppermute(array, 'col', pairs)  10.6 us
    all_to_all x1, waiting for transfers between devices, per_device(): lax.all_to_all(blocks, ('row', 'col'), 0, 0, tiled=True, axis_index_group...  9.83 us
    ppermute x5, starting transfers between devices, swap_core(): return lax.ppermute(array, 'row', [(i, i ^ 1) for i in range(2 * NZ)])  9.4 us
    all_to_all x1, starting transfers between devices, per_device(): lax.all_to_all(blocks, ('row', 'col'), 0, 0, tiled=True, axis_index_group...  8.52 us
    pallas_call x4, Pallas kernels, tile_products(): pl.pallas_call(functools.partial(tile_kernel, stage), in_specs=[smem] + [...  8.51 us
  transfers between devices with their start and end apart: 28, of which 11 were waited for; matrix products, arithmetic and copies ran while one was open for 1% of the time, Pallas kernels for 11%

profile of v2, /device:TPU:1, one launch (start us, length us, event | category | flops | bytes accessed | tf_op | source)
XLA Modules:
  0.0 110.7 jit_solution(12459730857387222752)
XLA Ops:
  1.7 2.1 %collective-permute-start.2 = (bf16[8,8192]{1,0:T(8,128)(2,1)S(1)}, bf16[8,8192]{1,0:T(8,128)(2,1)S(1)}, u32[]{:S(2)}, u32[]{:S(2)}) collective-permute-start(bf16[8,8192]{1,0:T(8,128)(2,1)S(1)} %get-tuple-element.47), channel_id=1, source_target_pairs={{0,1},{1,2},{2,3},{3,0},{4,5},{5,6},{6,7},{7,4},{8,9},{9,10},{10,1... | collective-permute-start | bytes 393224 | tf_op jit(solution)/shard_map/ppermute | solution.py:25
  3.8 2.5 %collective-permute-start.1 = (bf16[8,8192]{1,0:T(8,128)(2,1)S(1)}, bf16[8,8192]{1,0:T(8,128)(2,1)S(1)}, u32[]{:S(2)}, u32[]{:S(2)}) collective-permute-start(bf16[8,8192]{1,0:T(8,128)(2,1)S(1)} %get-tuple-element.47), channel_id=1, source_target_pairs={{0,2},{1,3},{2,0},{3,1},{4,6},{5,7},{6,4},{7,5},{8,10},{9,11},{10,... | collective-permute-start | bytes 393224 | tf_op jit(solution)/shard_map/ppermute | solution.py:25
  6.3 1.2 %collective-permute-start = (bf16[8,8192]{1,0:T(8,128)(2,1)S(1)}, bf16[8,8192]{1,0:T(8,128)(2,1)S(1)}, u32[]{:S(2)}, u32[]{:S(2)}) collective-permute-start(bf16[8,8192]{1,0:T(8,128)(2,1)S(1)} %get-tuple-element.47), channel_id=1, source_target_pairs={{0,3},{1,0},{2,1},{3,2},{4,7},{5,4},{6,5},{7,6},{8,11},{9,8},{10,9... | collective-permute-start | bytes 393224 | tf_op jit(solution)/shard_map/ppermute | solution.py:25
  7.4 1.3 %collective-permute-start.5 = (bf16[8,8192]{1,0:T(8,128)(2,1)S(1)}, bf16[8,8192]{1,0:T(8,128)(2,1)S(1)}, u32[]{:S(2)}, u32[]{:S(2)}) collective-permute-start(bf16[8,8192]{1,0:T(8,128)(2,1)S(1)} %get-tuple-element.46), channel_id=1, source_target_pairs={{0,4},{1,5},{2,6},{3,7},{4,8},{5,9},{6,10},{7,11},{8,12},{9,13},{1... | collective-permute-start | bytes 393224 | tf_op jit(solution)/shard_map/ppermute | solution.py:30
  8.7 2.6 %collective-permute-start.4 = (bf16[8,8192]{1,0:T(8,128)(2,1)S(1)}, bf16[8,8192]{1,0:T(8,128)(2,1)S(1)}, u32[]{:S(2)}, u32[]{:S(2)}) collective-permute-start(bf16[8,8192]{1,0:T(8,128)(2,1)S(1)} %get-tuple-element.46), channel_id=1, source_target_pairs={{0,8},{1,9},{2,10},{3,11},{4,12},{5,13},{6,14},{7,15},{8,0},{9,1},... | collective-permute-start | bytes 393224 | tf_op jit(solution)/shard_map/ppermute | solution.py:30
  12.8 3.1 %collective-permute-done.4 = bf16[8,8192]{1,0:T(8,128)(2,1)S(1)} collective-permute-done((bf16[8,8192]{1,0:T(8,128)(2,1)S(1)}, bf16[8,8192]{1,0:T(8,128)(2,1)S(1)}, u32[]{:S(2)}, u32[]{:S(2)}) %collective-permute-start.4) | collective-permute-done | bytes 131104 | tf_op jit(solution)/shard_map/ppermute | solution.py:30
  16.7 2.6 %collective-permute-start.7 = (bf16[32,8192]{1,0:T(8,128)(2,1)S(1)}, bf16[32,8192]{1,0:T(8,128)(2,1)S(1)}, u32[]{:S(2)}, u32[]{:S(2)}) collective-permute-start(bf16[32,8192]{1,0:T(8,128)(2,1)S(1)} %pad_maximum_fusion.refs_0_), channel_id=1, source_target_pairs={{0,12},{1,13},{2,14},{3,15},{4,0},{5,1},{6,2},{7,3},{8,4},{9,5},{1... | collective-permute-start | bytes 1572872 | tf_op jit(solution)/shard_map/ppermute | solution.py:30
  19.6 2.4 %collective-permute-start.11 = (bf16[32,8192]{1,0:T(8,128)(2,1)S(1)}, bf16[32,8192]{1,0:T(8,128)(2,1)S(1)}, u32[]{:S(2)}, u32[]{:S(2)}) collective-permute-start(bf16[32,8192]{1,0:T(8,128)(2,1)S(1)} %pad_maximum_fusion.1.refs_5_), channel_id=1, source_target_pairs={{0,3},{1,0},{2,1},{3,2},{4,7},{5,4},{6,5},{7,6},{8,11},{9,8},{10,9... | collective-permute-start | bytes 1572872 | tf_op jit(solution)/shard_map/ppermute | solution.py:25
  21.9 5.6 %collective-permute-start.6 = (bf16[512,256]{1,0:T(8,128)(2,1)}, bf16[512,256]{1,0:T(8,128)(2,1)S(1)}, u32[]{:S(2)}, u32[]{:S(2)}) collective-permute-start(bf16[512,256]{1,0:T(8,128)(2,1)} %feat_ref.1), channel_id=1, source_target_pairs={{0,224},{16,240},{32,0},{48,16},{64,32},{80,48},{96,64},{112,80},{... | collective-permute-start | bytes 786440 | tf_op jit(solution)/shard_map/ppermute | solution.py:35
  27.5 1.3 %collective-permute-done.8.refs_4_ = bf16[32,8192]{1,0:T(8,128)(2,1)S(1)} collective-permute-done((bf16[32,8192]{1,0:T(8,128)(2,1)S(1)}, bf16[32,8192]{1,0:T(8,128)(2,1)S(1)}, u32[]{:S(2)}, u32[]{:S(2)}) %collective-permute-start.8) | collective-permute-done | bytes 524320 | tf_op jit(solution)/shard_map/ppermute | solution.py:30
  28.9 2.7 %collective-permute-start.10 = (bf16[16,8192]{1,0:T(8,128)(2,1)S(1)}, bf16[16,8192]{1,0:T(8,128)(2,1)S(1)}, u32[]{:S(2)}, u32[]{:S(2)}) collective-permute-start(bf16[16,8192]{1,0:T(8,128)(2,1)S(1)} %slice.83), channel_id=1, source_target_pairs={{0,12},{1,13},{2,14},{3,15},{4,0},{5,1},{6,2},{7,3},{8,4},{9,5},{1... | collective-permute-start | bytes 786440 | tf_op jit(solution)/shard_map/ppermute | solution.py:30
  32.3 2.2 %collective-permute-start.14 = (bf16[16,8192]{1,0:T(8,128)(2,1)S(1)}, bf16[16,8192]{1,0:T(8,128)(2,1)S(1)}, u32[]{:S(2)}, u32[]{:S(2)}) collective-permute-start(bf16[16,8192]{1,0:T(8,128)(2,1)S(1)} %slice.85), channel_id=1, source_target_pairs={{0,3},{1,0},{2,1},{3,2},{4,7},{5,4},{6,5},{7,6},{8,11},{9,8},{10,9... | collective-permute-start | bytes 786440 | tf_op jit(solution)/shard_map/ppermute | solution.py:25
  35.9 4.0 %shard_map.86 = (s32[4,256]{1,0:T(4,128)S(1)}, bf16[256,256]{1,0:T(8,128)(2,1)S(1)}, bf16[320,128,128]{2,1,0:T(8,128)(2,1)S(1)}) custom-call(s32[1,320]{1,0:T(1,128)S(1)} %bitcast.50, s32[1,1]{1,0:T(1,128)S(6)} %copy.10.count_ref, bf16[320,128,128]{2,1,0:T(8,128)(2,1)} %bitcast.51), custom_call_target="tpu_custom_call" | custom-call | bytes 14000000 | tf_op jit(solution)/shard_map/pallas_call | solution.py:130
  39.9 1.9 %shard_map.87 = (bf16[2,256,512]{2,1,0:T(8,128)(2,1)S(1)}, bf16[2,256,512]{2,1,0:T(8,128)(2,1)S(1)}) custom-call(s32[4,256]{1,0:T(4,128)S(1)} %get-tuple-element.24.table_ref, bf16[32,8192]{1,0:T(8,128)(2,1)S(1)} %pad_maximum_fusion.refs_0_, bf16[32,8192]{1,0:T(8,128)(2,1)S(1)} %collective-permute-done.7.refs_1_, ...), custom_call_target="tpu_custom_call" | custom-call | bytes 1000000 | tf_op jit(solution)/shard_map/pallas_call | solution.py:198
  41.8 4.7 %collective-permute-start.15 = (bf16[2,256,512]{2,1,0:T(8,128)(2,1)S(1)}, bf16[2,256,512]{2,1,0:T(8,128)(2,1)S(1)}, u32[]{:S(2)}, u32[]{:S(2)}) collective-permute-start(bf16[2,256,512]{2,1,0:T(8,128)(2,1)S(1)} %get-tuple-element.29), channel_id=1, source_target_pairs={{0,16},{16,0},{32,48},{48,32},{64,80},{80,64},{96,112},{112,96},{1... | collective-permute-start | bytes 1572872 | tf_op jit(solution)/shard_map/ppermute | solution.py:39
  46.6 1.9 %shard_map.88 = (bf16[2,256,512]{2,1,0:T(8,128)(2,1)S(1)}, bf16[2,256,512]{2,1,0:T(8,128)(2,1)S(1)}) custom-call(s32[4,256]{1,0:T(4,128)S(1)} %get-tuple-element.24.table_ref, bf16[32,8192]{1,0:T(8,128)(2,1)S(1)} %pad_maximum_fusion.refs_0_, bf16[32,8192]{1,0:T(8,128)(2,1)S(1)} %collective-permute-done.7.refs_1_, ...), custom_call_target="tpu_custom_call" | custom-call | bytes 1000000 | tf_op jit(solution)/shard_map/pallas_call | solution.py:198
  48.7 10.7 %collective-permute-start.23 = (bf16[256,512]{1,0:T(8,128)(2,1)S(1)}, bf16[256,512]{1,0:T(8,128)(2,1)S(1)}, u32[]{:S(2)}, u32[]{:S(2)}) collective-permute-start(bf16[256,512]{1,0:T(8,128)(2,1)S(1)} %get-tuple-element.44), channel_id=1, source_target_pairs={{0,224},{16,240},{32,0},{48,16},{64,32},{80,48},{96,64},{112,80},{... | collective-permute-start | bytes 786440 | tf_op jit(solution)/shard_map/ppermute | solution.py:35
  59.5 2.5 %shard_map.89 = (bf16[2,256,512]{2,1,0:T(8,128)(2,1)S(1)}, bf16[2,256,512]{2,1,0:T(8,128)(2,1)S(1)}) custom-call(s32[4,256]{1,0:T(4,128)S(1)} %get-tuple-element.24.table_ref, bf16[32,8192]{1,0:T(8,128)(2,1)S(1)} %pad_maximum_fusion.refs_0_, bf16[32,8192]{1,0:T(8,128)(2,1)S(1)} %collective-permute-done.7.refs_1_, ...), custom_call_target="tpu_custom_call" | custom-call | bytes 1000000 | tf_op jit(solution)/shard_map/pallas_call | solution.py:198
  62.1 3.1 %collective-permute-done.23 = bf16[256,512]{1,0:T(8,128)(2,1)S(1)} collective-permute-done((bf16[256,512]{1,0:T(8,128)(2,1)S(1)}, bf16[256,512]{1,0:T(8,128)(2,1)S(1)}, u32[]{:S(2)}, u32[]{:S(2)}) %collective-permute-start.23) | collective-permute-done | bytes 262176 | tf_op jit(solution)/shard_map/ppermute | solution.py:35
  65.2 3.1 %collective-permute-done.16 = bf16[256,512]{1,0:T(8,128)(2,1)S(1)} collective-permute-done((bf16[256,512]{1,0:T(8,128)(2,1)S(1)}, bf16[256,512]{1,0:T(8,128)(2,1)S(1)}, u32[]{:S(2)}, u32[]{:S(2)}) %collective-permute-start.16) | collective-permute-done | bytes 262176 | tf_op jit(solution)/shard_map/ppermute | solution.py:35
  68.9 1.1 %collective-permute-start.18 = (bf16[256,512]{1,0:T(8,128)(2,1)S(1)}, bf16[256,512]{1,0:T(8,128)(2,1)S(1)}, u32[]{:S(2)}, u32[]{:S(2)}) collective-permute-start(bf16[256,512]{1,0:T(8,128)(2,1)S(1)} %get-tuple-element.43), channel_id=1, source_target_pairs={{0,32},{16,48},{32,64},{48,80},{64,96},{80,112},{96,128},{112,144}... | collective-permute-start | bytes 786440 | tf_op jit(solution)/shard_map/ppermute | solution.py:35
  70.0 2.2 %shard_map.90 = (bf16[2,256,512]{2,1,0:T(8,128)(2,1)S(1)}, bf16[2,256,512]{2,1,0:T(8,128)(2,1)S(1)}) custom-call(s32[4,256]{1,0:T(4,128)S(1)} %get-tuple-element.24.table_ref, bf16[32,8192]{1,0:T(8,128)(2,1)S(1)} %pad_maximum_fusion.refs_0_, bf16[32,8192]{1,0:T(8,128)(2,1)S(1)} %collective-permute-done.7.refs_1_, ...), custom_call_target="tpu_custom_call" | custom-call | bytes 1000000 | tf_op jit(solution)/shard_map/pallas_call | solution.py:198
  72.3 1.4 %collective-permute-start.21 = (bf16[2,256,512]{2,1,0:T(8,128)(2,1)S(1)}, bf16[2,256,512]{2,1,0:T(8,128)(2,1)S(1)}, u32[]{:S(2)}, u32[]{:S(2)}) collective-permute-start(bf16[2,256,512]{2,1,0:T(8,128)(2,1)S(1)} %get-tuple-element.35), channel_id=1, source_target_pairs={{0,16},{16,0},{32,48},{48,32},{64,80},{80,64},{96,112},{112,96},{1... | collective-permute-start | bytes 1572872 | tf_op jit(solution)/shard_map/ppermute | solution.py:39
  73.7 1.6 %collective-permute-done.24 = bf16[256,512]{1,0:T(8,128)(2,1)S(1)} collective-permute-done((bf16[256,512]{1,0:T(8,128)(2,1)S(1)}, bf16[256,512]{1,0:T(8,128)(2,1)S(1)}, u32[]{:S(2)}, u32[]{:S(2)}) %collective-permute-start.24) | collective-permute-done | bytes 262176 | tf_op jit(solution)/shard_map/ppermute | solution.py:35
  75.3 1.6 %collective-permute-done.18 = bf16[256,512]{1,0:T(8,128)(2,1)S(1)} collective-permute-done((bf16[256,512]{1,0:T(8,128)(2,1)S(1)}, bf16[256,512]{1,0:T(8,128)(2,1)S(1)}, u32[]{:S(2)}, u32[]{:S(2)}) %collective-permute-start.18) | collective-permute-done | bytes 262176 | tf_op jit(solution)/shard_map/ppermute | solution.py:35
  77.1 2.7 %collective-permute-start.25 = (bf16[256,512]{1,0:T(8,128)(2,1)S(1)}, bf16[256,512]{1,0:T(8,128)(2,1)S(1)}, u32[]{:S(2)}, u32[]{:S(2)}) collective-permute-start(bf16[256,512]{1,0:T(8,128)(2,1)S(1)} %get-tuple-element.40), channel_id=1, source_target_pairs={{0,224},{16,240},{32,0},{48,16},{64,32},{80,48},{96,64},{112,80},{... | collective-permute-start | bytes 786440 | tf_op jit(solution)/shard_map/ppermute | solution.py:35
  79.8 4.3 %collective-permute-done.20 = bf16[256,512]{1,0:T(8,128)(2,1)S(1)} collective-permute-done((bf16[256,512]{1,0:T(8,128)(2,1)S(1)}, bf16[256,512]{1,0:T(8,128)(2,1)S(1)}, u32[]{:S(2)}, u32[]{:S(2)}) %collective-permute-start.20) | collective-permute-done | bytes 262176 | tf_op jit(solution)/shard_map/ppermute | solution.py:35
  84.2 1.2 %shard_map.92 = (f32[128,256]{1,0:T(8,128)S(1)}, f32[128,256]{1,0:T(8,128)S(1)}) custom-call(bf16[256,512]{1,0:T(8,128)(2,1)S(1)} %fusion.2.sent_ref, bf16[256,512]{1,0:T(8,128)(2,1)S(1)} %collective-permute-done.25.left_ref, bf16[2,256,512]{2,1,0:T(8,128)(2,1)S(1)} %get-tuple-element.34.mine_ref, ...), custom_call_target="tpu_custom_call" | custom-call | bytes 1000000 | tf_op jit(solution)/shard_map/pallas_call | solution.py:277
  85.4 3.0 %collective-permute-start.26 = (f32[128,256]{1,0:T(8,128)S(1)}, f32[128,256]{1,0:T(8,128)S(1)}, u32[]{:S(2)}, u32[]{:S(2)}) collective-permute-start(f32[128,256]{1,0:T(8,128)S(1)} %get-tuple-element.39), channel_id=1, source_target_pairs={{0,16},{16,0},{32,48},{48,32},{64,80},{80,64},{96,112},{112,96},{1... | collective-permute-start | bytes 393224 | tf_op jit(solution)/shard_map/ppermute | solution.py:39
  90.2 8.5 %all-to-all-start = ((f32[128,1,256]{2,1,0:T(1,128)}), f32[128,1,256]{2,1,0:T(1,128)S(1)}, u32[]{:S(2)}, u32[]{:S(2)}) async-start(f32[128,1,256]{2,1,0:T(1,128)} %copy.9), calls=%async_computation | async-start | bytes 262144 | tf_op jit(solution)/shard_map/all_to_all | solution.py:317
  98.8 1.3 %shard_map.91 = bf16[512,256]{1,0:T(8,128)(2,1)} custom-call(bf16[256,512]{1,0:T(8,128)(2,1)S(1)} %collective-permute-done.22.right_ref, bf16[256,512]{1,0:T(8,128)(2,1)S(1)} %collective-permute-done.25.left_ref, bf16[2,256,512]{2,1,0:T(8,128)(2,1)S(1)} %get-tuple-element.34.mine_ref, bf16[2,256,512]{2,1,0:T(8,128)(2,1)S(1)} %collective-permute-done.21.other_ref, ...), custom_call_target="tpu_custom_call" | custom-call | bytes 1000000 | tf_op jit(solution)/shard_map/pallas_call | solution.py:225
  100.0 9.8 %all-to-all-done = f32[128,1,256]{2,1,0:T(1,128)S(1)} async-done(((f32[128,1,256]{2,1,0:T(1,128)}), f32[128,1,256]{2,1,0:T(1,128)S(1)}, u32[]{:S(2)}, u32[]{:S(2)}) %all-to-all-start) | async-done | bytes 131104 | tf_op jit(solution)/shard_map/all_to_all | solution.py:317
  (53 shorter events, 9.1 us)
Async XLA Ops:
  1.7 9.6 %collective-permute-start.2 = (bf16[8,8192]{1,0:T(8,128)(2,1)S(1)}, bf16[8,8192]{1,0:T(8,128)(2,1)S(1)}, u32[]{:S(2)}, u32[]{:S(2)}) collective-permute-start(bf16[8,8192]{1,0:T(8,128)(2,1)S(1)} %get-tuple-element.47), channel_id=1, source_target_pairs={{0,1},{1,2},{2,3},{3,0},{4,5},{5,6},{6,7},{7,4},{8,9},{9,10},{10,1... | collective-permute-start | bytes 393224 | tf_op jit(solution)/shard_map/ppermute | solution.py:25
  3.8 8.6 %collective-permute-start.1 = (bf16[8,8192]{1,0:T(8,128)(2,1)S(1)}, bf16[8,8192]{1,0:T(8,128)(2,1)S(1)}, u32[]{:S(2)}, u32[]{:S(2)}) collective-permute-start(bf16[8,8192]{1,0:T(8,128)(2,1)S(1)} %get-tuple-element.47), channel_id=1, source_target_pairs={{0,2},{1,3},{2,0},{3,1},{4,6},{5,7},{6,4},{7,5},{8,10},{9,11},{10,... | collective-permute-start | bytes 393224 | tf_op jit(solution)/shard_map/ppermute | solution.py:25
  6.3 6.2 %collective-permute-start = (bf16[8,8192]{1,0:T(8,128)(2,1)S(1)}, bf16[8,8192]{1,0:T(8,128)(2,1)S(1)}, u32[]{:S(2)}, u32[]{:S(2)}) collective-permute-start(bf16[8,8192]{1,0:T(8,128)(2,1)S(1)} %get-tuple-element.47), channel_id=1, source_target_pairs={{0,3},{1,0},{2,1},{3,2},{4,7},{5,4},{6,5},{7,6},{8,11},{9,8},{10,9... | collective-permute-start | bytes 393224 | tf_op jit(solution)/shard_map/ppermute | solution.py:25
  7.4 5.4 %collective-permute-start.5 = (bf16[8,8192]{1,0:T(8,128)(2,1)S(1)}, bf16[8,8192]{1,0:T(8,128)(2,1)S(1)}, u32[]{:S(2)}, u32[]{:S(2)}) collective-permute-start(bf16[8,8192]{1,0:T(8,128)(2,1)S(1)} %get-tuple-element.46), channel_id=1, source_target_pairs={{0,4},{1,5},{2,6},{3,7},{4,8},{5,9},{6,10},{7,11},{8,12},{9,13},{1... | collective-permute-start | bytes 393224 | tf_op jit(solution)/shard_map/ppermute | solution.py:30
  8.7 7.1 %collective-permute-start.4 = (bf16[8,8192]{1,0:T(8,128)(2,1)S(1)}, bf16[8,8192]{1,0:T(8,128)(2,1)S(1)}, u32[]{:S(2)}, u32[]{:S(2)}) collective-permute-start(bf16[8,8192]{1,0:T(8,128)(2,1)S(1)} %get-tuple-element.46), channel_id=1, source_target_pairs={{0,8},{1,9},{2,10},{3,11},{4,12},{5,13},{6,14},{7,15},{8,0},{9,1},... | collective-permute-start | bytes 393224 | tf_op jit(solution)/shard_map/ppermute | solution.py:30
  11.4 5.1 %collective-permute-start.3 = (bf16[8,8192]{1,0:T(8,128)(2,1)S(1)}, bf16[8,8192]{1,0:T(8,128)(2,1)S(1)}, u32[]{:S(2)}, u32[]{:S(2)}) collective-permute-start(bf16[8,8192]{1,0:T(8,128)(2,1)S(1)} %get-tuple-element.46), channel_id=1, source_target_pairs={{0,12},{1,13},{2,14},{3,15},{4,0},{5,1},{6,2},{7,3},{8,4},{9,5},{1... | collective-permute-start | bytes 393224 | tf_op jit(solution)/shard_map/ppermute | solution.py:30
  16.5 12.3 %collective-permute-start.8 = (bf16[32,8192]{1,0:T(8,128)(2,1)S(1)}, bf16[32,8192]{1,0:T(8,128)(2,1)S(1)}, u32[]{:S(2)}, u32[]{:S(2)}) collective-permute-start(bf16[32,8192]{1,0:T(8,128)(2,1)S(1)} %pad_maximum_fusion.refs_0_), channel_id=1, source_target_pairs={{0,4},{1,5},{2,6},{3,7},{4,8},{5,9},{6,10},{7,11},{8,12},{9,13},{1... | collective-permute-start | bytes 1572872 | tf_op jit(solution)/shard_map/ppermute | solution.py:30
  16.7 12.2 %collective-permute-start.7 = (bf16[32,8192]{1,0:T(8,128)(2,1)S(1)}, bf16[32,8192]{1,0:T(8,128)(2,1)S(1)}, u32[]{:S(2)}, u32[]{:S(2)}) collective-permute-start(bf16[32,8192]{1,0:T(8,128)(2,1)S(1)} %pad_maximum_fusion.refs_0_), channel_id=1, source_target_pairs={{0,12},{1,13},{2,14},{3,15},{4,0},{5,1},{6,2},{7,3},{8,4},{9,5},{1... | collective-permute-start | bytes 1572872 | tf_op jit(solution)/shard_map/ppermute | solution.py:30
  19.3 12.4 %collective-permute-start.12 = (bf16[32,8192]{1,0:T(8,128)(2,1)S(1)}, bf16[32,8192]{1,0:T(8,128)(2,1)S(1)}, u32[]{:S(2)}, u32[]{:S(2)}) collective-permute-start(bf16[32,8192]{1,0:T(8,128)(2,1)S(1)} %pad_maximum_fusion.1.refs_5_), channel_id=1, source_target_pairs={{0,1},{1,2},{2,3},{3,0},{4,5},{5,6},{6,7},{7,4},{8,9},{9,10},{10,1... | collective-permute-start | bytes 1572872 | tf_op jit(solution)/shard_map/ppermute | solution.py:25
  19.6 12.7 %collective-permute-start.11 = (bf16[32,8192]{1,0:T(8,128)(2,1)S(1)}, bf16[32,8192]{1,0:T(8,128)(2,1)S(1)}, u32[]{:S(2)}, u32[]{:S(2)}) collective-permute-start(bf16[32,8192]{1,0:T(8,128)(2,1)S(1)} %pad_maximum_fusion.1.refs_5_), channel_id=1, source_target_pairs={{0,3},{1,0},{2,1},{3,2},{4,7},{5,4},{6,5},{7,6},{8,11},{9,8},{10,9... | collective-permute-start | bytes 1572872 | tf_op jit(solution)/shard_map/ppermute | solution.py:25
  21.9 18.0 %collective-permute-start.6 = (bf16[512,256]{1,0:T(8,128)(2,1)}, bf16[512,256]{1,0:T(8,128)(2,1)S(1)}, u32[]{:S(2)}, u32[]{:S(2)}) collective-permute-start(bf16[512,256]{1,0:T(8,128)(2,1)} %feat_ref.1), channel_id=1, source_target_pairs={{0,224},{16,240},{32,0},{48,16},{64,32},{80,48},{96,64},{112,80},{... | collective-permute-start | bytes 786440 | tf_op jit(solution)/shard_map/ppermute | solution.py:35
  28.8 11.1 %collective-permute-start.9 = (bf16[16,8192]{1,0:T(8,128)(2,1)S(1)}, bf16[16,8192]{1,0:T(8,128)(2,1)S(1)}, u32[]{:S(2)}, u32[]{:S(2)}) collective-permute-start(bf16[16,8192]{1,0:T(8,128)(2,1)S(1)} %slice.82), channel_id=1, source_target_pairs={{0,4},{1,5},{2,6},{3,7},{4,8},{5,9},{6,10},{7,11},{8,12},{9,13},{1... | collective-permute-start | bytes 786440 | tf_op jit(solution)/shard_map/ppermute | solution.py:30
  28.9 11.0 %collective-permute-start.10 = (bf16[16,8192]{1,0:T(8,128)(2,1)S(1)}, bf16[16,8192]{1,0:T(8,128)(2,1)S(1)}, u32[]{:S(2)}, u32[]{:S(2)}) collective-permute-start(bf16[16,8192]{1,0:T(8,128)(2,1)S(1)} %slice.83), channel_id=1, source_target_pairs={{0,12},{1,13},{2,14},{3,15},{4,0},{5,1},{6,2},{7,3},{8,4},{9,5},{1... | collective-permute-start | bytes 786440 | tf_op jit(solution)/shard_map/ppermute | solution.py:30
  31.7 8.2 %collective-permute-start.13 = (bf16[16,8192]{1,0:T(8,128)(2,1)S(1)}, bf16[16,8192]{1,0:T(8,128)(2,1)S(1)}, u32[]{:S(2)}, u32[]{:S(2)}) collective-permute-start(bf16[16,8192]{1,0:T(8,128)(2,1)S(1)} %slice.84), channel_id=1, source_target_pairs={{0,1},{1,2},{2,3},{3,0},{4,5},{5,6},{6,7},{7,4},{8,9},{9,10},{10,1... | collective-permute-start | bytes 786440 | tf_op jit(solution)/shard_map/ppermute | solution.py:25
  32.3 7.6 %collective-permute-start.14 = (bf16[16,8192]{1,0:T(8,128)(2,1)S(1)}, bf16[16,8192]{1,0:T(8,128)(2,1)S(1)}, u32[]{:S(2)}, u32[]{:S(2)}) collective-permute-start(bf16[16,8192]{1,0:T(8,128)(2,1)S(1)} %slice.85), channel_id=1, source_target_pairs={{0,3},{1,0},{2,1},{3,2},{4,7},{5,4},{6,5},{7,6},{8,11},{9,8},{10,9... | collective-permute-start | bytes 786440 | tf_op jit(solution)/shard_map/ppermute | solution.py:25
  35.2 0.7 copy-start.2
  41.8 6.8 %collective-permute-start.15 = (bf16[2,256,512]{2,1,0:T(8,128)(2,1)S(1)}, bf16[2,256,512]{2,1,0:T(8,128)(2,1)S(1)}, u32[]{:S(2)}, u32[]{:S(2)}) collective-permute-start(bf16[2,256,512]{2,1,0:T(8,128)(2,1)S(1)} %get-tuple-element.29), channel_id=1, source_target_pairs={{0,16},{16,0},{32,48},{48,32},{64,80},{80,64},{96,112},{112,96},{1... | collective-permute-start | bytes 1572872 | tf_op jit(solution)/shard_map/ppermute | solution.py:39
  48.5 13.6 %collective-permute-start.17 = (bf16[2,256,512]{2,1,0:T(8,128)(2,1)S(1)}, bf16[2,256,512]{2,1,0:T(8,128)(2,1)S(1)}, u32[]{:S(2)}, u32[]{:S(2)}) collective-permute-start(bf16[2,256,512]{2,1,0:T(8,128)(2,1)S(1)} %get-tuple-element.31), channel_id=1, source_target_pairs={{0,16},{16,0},{32,48},{48,32},{64,80},{80,64},{96,112},{112,96},{1... | collective-permute-start | bytes 1572872 | tf_op jit(solution)/shard_map/ppermute | solution.py:39
  48.7 16.4 %collective-permute-start.23 = (bf16[256,512]{1,0:T(8,128)(2,1)S(1)}, bf16[256,512]{1,0:T(8,128)(2,1)S(1)}, u32[]{:S(2)}, u32[]{:S(2)}) collective-permute-start(bf16[256,512]{1,0:T(8,128)(2,1)S(1)} %get-tuple-element.44), channel_id=1, source_target_pairs={{0,224},{16,240},{32,0},{48,16},{64,32},{80,48},{96,64},{112,80},{... | collective-permute-start | bytes 786440 | tf_op jit(solution)/shard_map/ppermute | solution.py:35
  59.5 8.8 %collective-permute-start.16 = (bf16[256,512]{1,0:T(8,128)(2,1)S(1)}, bf16[256,512]{1,0:T(8,128)(2,1)S(1)}, u32[]{:S(2)}, u32[]{:S(2)}) collective-permute-start(bf16[256,512]{1,0:T(8,128)(2,1)S(1)} %get-tuple-element.45), channel_id=1, source_target_pairs={{0,32},{16,48},{32,64},{48,80},{64,96},{80,112},{96,128},{112,144}... | collective-permute-start | bytes 786440 | tf_op jit(solution)/shard_map/ppermute | solution.py:35
  62.0 22.2 %copy-start = (bf16[512,256]{1,0:T(8,128)(2,1)S(1)}, bf16[512,256]{1,0:T(8,128)(2,1)}, u32[]{:S(2)}) copy-start(bf16[512,256]{1,0:T(8,128)(2,1)} %feat_ref.1) | copy-start | bytes 786436
  62.0 11.7 %collective-permute-start.19 = (bf16[2,256,512]{2,1,0:T(8,128)(2,1)S(1)}, bf16[2,256,512]{2,1,0:T(8,128)(2,1)S(1)}, u32[]{:S(2)}, u32[]{:S(2)}) collective-permute-start(bf16[2,256,512]{2,1,0:T(8,128)(2,1)S(1)} %get-tuple-element.33), channel_id=1, source_target_pairs={{0,16},{16,0},{32,48},{48,32},{64,80},{80,64},{96,112},{112,96},{1... | collective-permute-start | bytes 1572872 | tf_op jit(solution)/shard_map/ppermute | solution.py:39
  68.5 6.8 %collective-permute-start.24 = (bf16[256,512]{1,0:T(8,128)(2,1)S(1)}, bf16[256,512]{1,0:T(8,128)(2,1)S(1)}, u32[]{:S(2)}, u32[]{:S(2)}) collective-permute-start(bf16[256,512]{1,0:T(8,128)(2,1)S(1)} %get-tuple-element.42), channel_id=1, source_target_pairs={{0,224},{16,240},{32,0},{48,16},{64,32},{80,48},{96,64},{112,80},{... | collective-permute-start | bytes 786440 | tf_op jit(solution)/shard_map/ppermute | solution.py:35
  68.9 29.9 %copy-start.1 = (bf16[256,256]{1,0:T(8,128)(2,1)S(1)}, bf16[256,256]{1,0:T(8,128)(2,1)}, u32[]{:S(2)}) copy-start(bf16[256,256]{1,0:T(8,128)(2,1)} %weight_ref.1) | copy-start | bytes 393220
  68.9 7.9 %collective-permute-start.18 = (bf16[256,512]{1,0:T(8,128)(2,1)S(1)}, bf16[256,512]{1,0:T(8,128)(2,1)S(1)}, u32[]{:S(2)}, u32[]{:S(2)}) collective-permute-start(bf16[256,512]{1,0:T(8,128)(2,1)S(1)} %get-tuple-element.43), channel_id=1, source_target_pairs={{0,32},{16,48},{32,64},{48,80},{64,96},{80,112},{96,128},{112,144}... | collective-permute-start | bytes 786440 | tf_op jit(solution)/shard_map/ppermute | solution.py:35
  72.3 7.5 %collective-permute-start.21 = (bf16[2,256,512]{2,1,0:T(8,128)(2,1)S(1)}, bf16[2,256,512]{2,1,0:T(8,128)(2,1)S(1)}, u32[]{:S(2)}, u32[]{:S(2)}) collective-permute-start(bf16[2,256,512]{2,1,0:T(8,128)(2,1)S(1)} %get-tuple-element.35), channel_id=1, source_target_pairs={{0,16},{16,0},{32,48},{48,32},{64,80},{80,64},{96,112},{112,96},{1... | collective-permute-start | bytes 1572872 | tf_op jit(solution)/shard_map/ppermute | solution.py:39
  77.0 7.1 %collective-permute-start.20 = (bf16[256,512]{1,0:T(8,128)(2,1)S(1)}, bf16[256,512]{1,0:T(8,128)(2,1)S(1)}, u32[]{:S(2)}, u32[]{:S(2)}) collective-permute-start(bf16[256,512]{1,0:T(8,128)(2,1)S(1)} %get-tuple-element.41), channel_id=1, source_target_pairs={{0,32},{16,48},{32,64},{48,80},{64,96},{80,112},{96,128},{112,144}... | collective-permute-start | bytes 786440 | tf_op jit(solution)/shard_map/ppermute | solution.py:35
  77.1 7.1 %collective-permute-start.25 = (bf16[256,512]{1,0:T(8,128)(2,1)S(1)}, bf16[256,512]{1,0:T(8,128)(2,1)S(1)}, u32[]{:S(2)}, u32[]{:S(2)}) collective-permute-start(bf16[256,512]{1,0:T(8,128)(2,1)S(1)} %get-tuple-element.40), channel_id=1, source_target_pairs={{0,224},{16,240},{32,0},{48,16},{64,32},{80,48},{96,64},{112,80},{... | collective-permute-start | bytes 786440 | tf_op jit(solution)/shard_map/ppermute | solution.py:35
  85.4 4.0 %collective-permute-start.26 = (f32[128,256]{1,0:T(8,128)S(1)}, f32[128,256]{1,0:T(8,128)S(1)}, u32[]{:S(2)}, u32[]{:S(2)}) collective-permute-start(f32[128,256]{1,0:T(8,128)S(1)} %get-tuple-element.39), channel_id=1, source_target_pairs={{0,16},{16,0},{32,48},{48,32},{64,80},{80,64},{96,112},{112,96},{1... | collective-permute-start | bytes 393224 | tf_op jit(solution)/shard_map/ppermute | solution.py:39
  88.4 10.3 %collective-permute-start.22 = (bf16[256,512]{1,0:T(8,128)(2,1)S(1)}, bf16[256,512]{1,0:T(8,128)(2,1)S(1)}, u32[]{:S(2)}, u32[]{:S(2)}) collective-permute-start(bf16[256,512]{1,0:T(8,128)(2,1)S(1)} %fusion.2.sent_ref), channel_id=1, source_target_pairs={{0,32},{16,48},{32,64},{48,80},{64,96},{80,112},{96,128},{112,144}... | collective-permute-start | bytes 786440 | tf_op jit(solution)/shard_map/ppermute | solution.py:35
  90.2 19.7 %all-to-all-start = ((f32[128,1,256]{2,1,0:T(1,128)}), f32[128,1,256]{2,1,0:T(1,128)S(1)}, u32[]{:S(2)}, u32[]{:S(2)}) async-start(f32[128,1,256]{2,1,0:T(1,128)} %copy.9), calls=%async_computation | async-start | bytes 262144 | tf_op jit(solution)/shard_map/all_to_all | solution.py:317

commit v3 on v2

--- a/solution.py
+++ b/solution.py
@@ -16,7 +16,7 @@
 COLS = 64
 STAGES = 4
 STAGE_COLS = COLS // STAGES
-GROUP = 4
+GROUP = 8
 VMEM_LIMIT = 20 * 1024 * 1024
 
 

time: 110 us -> 109 us (level)
  waiting for transfers between devices: 29.7 us -> 27.4 us
  Pallas kernels: 15 us -> 17.2 us
  starting transfers between devices: 60.3 us -> 58.6 us
    ppermute x8, starting transfers between devices: 20.6 us -> 16 us  [shift_z(): return lax.ppermute(array, 'row', pairs)]
    ppermute x8, waiting for transfers between devices: 13.6 us -> 11.3 us  [shift_z(): return lax.ppermute(array, 'row', pairs)]
    pallas_call x4, Pallas kernels: 8.51 us -> 10.8 us  [tile_products(): pl.pallas_call(functools.partial(tile_kernel, stage), in_specs=[smem] + [...]
    all_to_all x1, starting transfers between devices: 8.52 us -> 10.5 us  [per_device(): lax.all_to_all(blocks, ('row', 'col'), 0, 0, tiled=True, axis_index_group...]
  transfers between devices with their start and end apart: 28 -> 28, of which waited for: 11 -> 11; matrix products, arithmetic and copies ran while one was open for 1% -> 1% of each run, Pallas kernels for 11% -> 12%
where the time goes in v3:
time: 109 us
  starting transfers between devices  58.6 us (54%)
  waiting for transfers between devices  27.4 us (25%)
  Pallas kernels  17.2 us (16%)
  local copies, waits for them, and re-layouts  2.23 us (2%)
  other arithmetic  1.96 us (2%)
  between operations  1.55 us (1%)
    ppermute x8, starting transfers between devices, shift_z(): return lax.ppermute(array, 'row', pairs)  16 us
    ppermute x8, waiting for transfers between devices, shift_z(): return lax.ppermute(array, 'row', pairs)  11.3 us
    ppermute x7, starting transfers between devices, shift_x(): return lax.ppermute(array, 'col', pairs)  11.2 us
    pallas_call x4, Pallas kernels, tile_products(): pl.pallas_call(functools.partial(tile_kernel, stage), in_specs=[smem] + [...  10.8 us
    ppermute x7, starting transfers between devices, shift_y(): return lax.ppermute(array, 'col', pairs)  10.6 us
    all_to_all x1, starting transfers between devices, per_device(): lax.all_to_all(blocks, ('row', 'col'), 0, 0, tiled=True, axis_index_group...  10.5 us
    ppermute x5, starting transfers between devices, swap_core(): return lax.ppermute(array, 'row', [(i, i ^ 1) for i in range(2 * NZ)])  10.3 us
    all_to_all x1, waiting for transfers between devices, per_device(): lax.all_to_all(blocks, ('row', 'col'), 0, 0, tiled=True, axis_index_group...  9.83 us
  transfers between devices with their start and end apart: 28, of which 11 were waited for; matrix products, arithmetic and copies ran while one was open for 1% of the time, Pallas kernels for 12%

profile of v3, /device:TPU:1, one launch (start us, length us, event | category | flops | bytes accessed | tf_op | source)
XLA Modules:
  0.0 109.0 jit_solution(11381366567512151484)
XLA Ops:
  0.6 1.1 fusion.5
  1.7 2.1 %collective-permute-start.2 = (bf16[8,8192]{1,0:T(8,128)(2,1)S(1)}, bf16[8,8192]{1,0:T(8,128)(2,1)S(1)}, u32[]{:S(2)}, u32[]{:S(2)}) collective-permute-start(bf16[8,8192]{1,0:T(8,128)(2,1)S(1)} %get-tuple-element.47), channel_id=1, source_target_pairs={{0,1},{1,2},{2,3},{3,0},{4,5},{5,6},{6,7},{7,4},{8,9},{9,10},{10,1... | collective-permute-start | bytes 393224 | tf_op jit(solution)/shard_map/ppermute | solution.py:25
  3.8 2.5 %collective-permute-start.1 = (bf16[8,8192]{1,0:T(8,128)(2,1)S(1)}, bf16[8,8192]{1,0:T(8,128)(2,1)S(1)}, u32[]{:S(2)}, u32[]{:S(2)}) collective-permute-start(bf16[8,8192]{1,0:T(8,128)(2,1)S(1)} %get-tuple-element.47), channel_id=1, source_target_pairs={{0,2},{1,3},{2,0},{3,1},{4,6},{5,7},{6,4},{7,5},{8,10},{9,11},{10,... | collective-permute-start | bytes 393224 | tf_op jit(solution)/shard_map/ppermute | solution.py:25
  6.3 1.2 %collective-permute-start = (bf16[8,8192]{1,0:T(8,128)(2,1)S(1)}, bf16[8,8192]{1,0:T(8,128)(2,1)S(1)}, u32[]{:S(2)}, u32[]{:S(2)}) collective-permute-start(bf16[8,8192]{1,0:T(8,128)(2,1)S(1)} %get-tuple-element.47), channel_id=1, source_target_pairs={{0,3},{1,0},{2,1},{3,2},{4,7},{5,4},{6,5},{7,6},{8,11},{9,8},{10,9... | collective-permute-start | bytes 393224 | tf_op jit(solution)/shard_map/ppermute | solution.py:25
  7.4 1.3 %collective-permute-start.5 = (bf16[8,8192]{1,0:T(8,128)(2,1)S(1)}, bf16[8,8192]{1,0:T(8,128)(2,1)S(1)}, u32[]{:S(2)}, u32[]{:S(2)}) collective-permute-start(bf16[8,8192]{1,0:T(8,128)(2,1)S(1)} %get-tuple-element.46), channel_id=1, source_target_pairs={{0,4},{1,5},{2,6},{3,7},{4,8},{5,9},{6,10},{7,11},{8,12},{9,13},{1... | collective-permute-start | bytes 393224 | tf_op jit(solution)/shard_map/ppermute | solution.py:30
  8.7 2.6 %collective-permute-start.4 = (bf16[8,8192]{1,0:T(8,128)(2,1)S(1)}, bf16[8,8192]{1,0:T(8,128)(2,1)S(1)}, u32[]{:S(2)}, u32[]{:S(2)}) collective-permute-start(bf16[8,8192]{1,0:T(8,128)(2,1)S(1)} %get-tuple-element.46), channel_id=1, source_target_pairs={{0,8},{1,9},{2,10},{3,11},{4,12},{5,13},{6,14},{7,15},{8,0},{9,1},... | collective-permute-start | bytes 393224 | tf_op jit(solution)/shard_map/ppermute | solution.py:30
  11.4 1.1 collective-permute-start.3
  12.8 3.1 %collective-permute-done.4 = bf16[8,8192]{1,0:T(8,128)(2,1)S(1)} collective-permute-done((bf16[8,8192]{1,0:T(8,128)(2,1)S(1)}, bf16[8,8192]{1,0:T(8,128)(2,1)S(1)}, u32[]{:S(2)}, u32[]{:S(2)}) %collective-permute-start.4) | collective-permute-done | bytes 131104 | tf_op jit(solution)/shard_map/ppermute | solution.py:30
  16.7 2.6 %collective-permute-start.7 = (bf16[32,8192]{1,0:T(8,128)(2,1)S(1)}, bf16[32,8192]{1,0:T(8,128)(2,1)S(1)}, u32[]{:S(2)}, u32[]{:S(2)}) collective-permute-start(bf16[32,8192]{1,0:T(8,128)(2,1)S(1)} %pad_maximum_fusion.refs_0_), channel_id=1, source_target_pairs={{0,12},{1,13},{2,14},{3,15},{4,0},{5,1},{6,2},{7,3},{8,4},{9,5},{1... | collective-permute-start | bytes 1572872 | tf_op jit(solution)/shard_map/ppermute | solution.py:30
  19.6 2.4 %collective-permute-start.11 = (bf16[32,8192]{1,0:T(8,128)(2,1)S(1)}, bf16[32,8192]{1,0:T(8,128)(2,1)S(1)}, u32[]{:S(2)}, u32[]{:S(2)}) collective-permute-start(bf16[32,8192]{1,0:T(8,128)(2,1)S(1)} %pad_maximum_fusion.1.refs_5_), channel_id=1, source_target_pairs={{0,3},{1,0},{2,1},{3,2},{4,7},{5,4},{6,5},{7,6},{8,11},{9,8},{10,9... | collective-permute-start | bytes 1572872 | tf_op jit(solution)/shard_map/ppermute | solution.py:25
  21.9 5.6 %collective-permute-start.6 = (bf16[512,256]{1,0:T(8,128)(2,1)}, bf16[512,256]{1,0:T(8,128)(2,1)S(1)}, u32[]{:S(2)}, u32[]{:S(2)}) collective-permute-start(bf16[512,256]{1,0:T(8,128)(2,1)} %feat_ref.1), channel_id=1, source_target_pairs={{0,224},{16,240},{32,0},{48,16},{64,32},{80,48},{96,64},{112,80},{... | collective-permute-start | bytes 786440 | tf_op jit(solution)/shard_map/ppermute | solution.py:35
  27.5 1.3 %collective-permute-done.8.refs_4_ = bf16[32,8192]{1,0:T(8,128)(2,1)S(1)} collective-permute-done((bf16[32,8192]{1,0:T(8,128)(2,1)S(1)}, bf16[32,8192]{1,0:T(8,128)(2,1)S(1)}, u32[]{:S(2)}, u32[]{:S(2)}) %collective-permute-start.8) | collective-permute-done | bytes 524320 | tf_op jit(solution)/shard_map/ppermute | solution.py:30
  28.9 2.7 %collective-permute-start.10 = (bf16[16,8192]{1,0:T(8,128)(2,1)S(1)}, bf16[16,8192]{1,0:T(8,128)(2,1)S(1)}, u32[]{:S(2)}, u32[]{:S(2)}) collective-permute-start(bf16[16,8192]{1,0:T(8,128)(2,1)S(1)} %slice.83), channel_id=1, source_target_pairs={{0,12},{1,13},{2,14},{3,15},{4,0},{5,1},{6,2},{7,3},{8,4},{9,5},{1... | collective-permute-start | bytes 786440 | tf_op jit(solution)/shard_map/ppermute | solution.py:30
  32.3 2.2 %collective-permute-start.14 = (bf16[16,8192]{1,0:T(8,128)(2,1)S(1)}, bf16[16,8192]{1,0:T(8,128)(2,1)S(1)}, u32[]{:S(2)}, u32[]{:S(2)}) collective-permute-start(bf16[16,8192]{1,0:T(8,128)(2,1)S(1)} %slice.85), channel_id=1, source_target_pairs={{0,3},{1,0},{2,1},{3,2},{4,7},{5,4},{6,5},{7,6},{8,11},{9,8},{10,9... | collective-permute-start | bytes 786440 | tf_op jit(solution)/shard_map/ppermute | solution.py:25
  35.9 4.0 %shard_map.86 = (s32[4,256]{1,0:T(4,128)S(1)}, bf16[256,256]{1,0:T(8,128)(2,1)S(1)}, bf16[320,128,128]{2,1,0:T(8,128)(2,1)S(1)}) custom-call(s32[1,320]{1,0:T(1,128)S(1)} %bitcast.50, s32[1,1]{1,0:T(1,128)S(6)} %copy.10.count_ref, bf16[320,128,128]{2,1,0:T(8,128)(2,1)} %bitcast.51), custom_call_target="tpu_custom_call" | custom-call | bytes 14000000 | tf_op jit(solution)/shard_map/pallas_call | solution.py:130
  39.9 2.6 %shard_map.87 = (bf16[2,256,512]{2,1,0:T(8,128)(2,1)S(1)}, bf16[2,256,512]{2,1,0:T(8,128)(2,1)S(1)}) custom-call(s32[4,256]{1,0:T(4,128)S(1)} %get-tuple-element.24.table_ref, bf16[32,8192]{1,0:T(8,128)(2,1)S(1)} %pad_maximum_fusion.refs_0_, bf16[32,8192]{1,0:T(8,128)(2,1)S(1)} %collective-permute-done.7.refs_1_, ...), custom_call_target="tpu_custom_call" | custom-call | bytes 1000000 | tf_op jit(solution)/shard_map/pallas_call | solution.py:198
  42.6 4.5 %collective-permute-start.15 = (bf16[2,256,512]{2,1,0:T(8,128)(2,1)S(1)}, bf16[2,256,512]{2,1,0:T(8,128)(2,1)S(1)}, u32[]{:S(2)}, u32[]{:S(2)}) collective-permute-start(bf16[2,256,512]{2,1,0:T(8,128)(2,1)S(1)} %get-tuple-element.29), channel_id=1, source_target_pairs={{0,16},{16,0},{32,48},{48,32},{64,80},{80,64},{96,112},{112,96},{1... | collective-permute-start | bytes 1572872 | tf_op jit(solution)/shard_map/ppermute | solution.py:39
  47.1 2.9 %shard_map.88 = (bf16[2,256,512]{2,1,0:T(8,128)(2,1)S(1)}, bf16[2,256,512]{2,1,0:T(8,128)(2,1)S(1)}) custom-call(s32[4,256]{1,0:T(4,128)S(1)} %get-tuple-element.24.table_ref, bf16[32,8192]{1,0:T(8,128)(2,1)S(1)} %pad_maximum_fusion.refs_0_, bf16[32,8192]{1,0:T(8,128)(2,1)S(1)} %collective-permute-done.7.refs_1_, ...), custom_call_target="tpu_custom_call" | custom-call | bytes 1000000 | tf_op jit(solution)/shard_map/pallas_call | solution.py:198
  50.3 6.1 %collective-permute-start.23 = (bf16[256,512]{1,0:T(8,128)(2,1)S(1)}, bf16[256,512]{1,0:T(8,128)(2,1)S(1)}, u32[]{:S(2)}, u32[]{:S(2)}) collective-permute-start(bf16[256,512]{1,0:T(8,128)(2,1)S(1)} %get-tuple-element.44), channel_id=1, source_target_pairs={{0,224},{16,240},{32,0},{48,16},{64,32},{80,48},{96,64},{112,80},{... | collective-permute-start | bytes 786440 | tf_op jit(solution)/shard_map/ppermute | solution.py:35
  56.4 2.9 %shard_map.89 = (bf16[2,256,512]{2,1,0:T(8,128)(2,1)S(1)}, bf16[2,256,512]{2,1,0:T(8,128)(2,1)S(1)}) custom-call(s32[4,256]{1,0:T(4,128)S(1)} %get-tuple-element.24.table_ref, bf16[32,8192]{1,0:T(8,128)(2,1)S(1)} %pad_maximum_fusion.refs_0_, bf16[32,8192]{1,0:T(8,128)(2,1)S(1)} %collective-permute-done.7.refs_1_, ...), custom_call_target="tpu_custom_call" | custom-call | bytes 1000000 | tf_op jit(solution)/shard_map/pallas_call | solution.py:198
  59.4 2.2 %collective-permute-done.23 = bf16[256,512]{1,0:T(8,128)(2,1)S(1)} collective-permute-done((bf16[256,512]{1,0:T(8,128)(2,1)S(1)}, bf16[256,512]{1,0:T(8,128)(2,1)S(1)}, u32[]{:S(2)}, u32[]{:S(2)}) %collective-permute-start.23) | collective-permute-done | bytes 262176 | tf_op jit(solution)/shard_map/ppermute | solution.py:35
  61.6 3.1 %collective-permute-done.16 = bf16[256,512]{1,0:T(8,128)(2,1)S(1)} collective-permute-done((bf16[256,512]{1,0:T(8,128)(2,1)S(1)}, bf16[256,512]{1,0:T(8,128)(2,1)S(1)}, u32[]{:S(2)}, u32[]{:S(2)}) %collective-permute-start.16) | collective-permute-done | bytes 262176 | tf_op jit(solution)/shard_map/ppermute | solution.py:35
  66.4 2.4 %shard_map.90 = (bf16[2,256,512]{2,1,0:T(8,128)(2,1)S(1)}, bf16[2,256,512]{2,1,0:T(8,128)(2,1)S(1)}) custom-call(s32[4,256]{1,0:T(4,128)S(1)} %get-tuple-element.24.table_ref, bf16[32,8192]{1,0:T(8,128)(2,1)S(1)} %pad_maximum_fusion.refs_0_, bf16[32,8192]{1,0:T(8,128)(2,1)S(1)} %collective-permute-done.7.refs_1_, ...), custom_call_target="tpu_custom_call" | custom-call | bytes 1000000 | tf_op jit(solution)/shard_map/pallas_call | solution.py:198
  68.9 1.8 %collective-permute-start.21 = (bf16[2,256,512]{2,1,0:T(8,128)(2,1)S(1)}, bf16[2,256,512]{2,1,0:T(8,128)(2,1)S(1)}, u32[]{:S(2)}, u32[]{:S(2)}) collective-permute-start(bf16[2,256,512]{2,1,0:T(8,128)(2,1)S(1)} %get-tuple-element.35), channel_id=1, source_target_pairs={{0,16},{16,0},{32,48},{48,32},{64,80},{80,64},{96,112},{112,96},{1... | collective-permute-start | bytes 1572872 | tf_op jit(solution)/shard_map/ppermute | solution.py:39
  71.1 1.8 %collective-permute-done.18 = bf16[256,512]{1,0:T(8,128)(2,1)S(1)} collective-permute-done((bf16[256,512]{1,0:T(8,128)(2,1)S(1)}, bf16[256,512]{1,0:T(8,128)(2,1)S(1)}, u32[]{:S(2)}, u32[]{:S(2)}) %collective-permute-start.18) | collective-permute-done | bytes 262176 | tf_op jit(solution)/shard_map/ppermute | solution.py:35
  73.2 2.7 %collective-permute-start.25 = (bf16[256,512]{1,0:T(8,128)(2,1)S(1)}, bf16[256,512]{1,0:T(8,128)(2,1)S(1)}, u32[]{:S(2)}, u32[]{:S(2)}) collective-permute-start(bf16[256,512]{1,0:T(8,128)(2,1)S(1)} %get-tuple-element.40), channel_id=1, source_target_pairs={{0,224},{16,240},{32,0},{48,16},{64,32},{80,48},{96,64},{112,80},{... | collective-permute-start | bytes 786440 | tf_op jit(solution)/shard_map/ppermute | solution.py:35
  75.9 3.8 %collective-permute-done.20 = bf16[256,512]{1,0:T(8,128)(2,1)S(1)} collective-permute-done((bf16[256,512]{1,0:T(8,128)(2,1)S(1)}, bf16[256,512]{1,0:T(8,128)(2,1)S(1)}, u32[]{:S(2)}, u32[]{:S(2)}) %collective-permute-start.20) | collective-permute-done | bytes 262176 | tf_op jit(solution)/shard_map/ppermute | solution.py:35
  79.8 1.2 %shard_map.92 = (f32[128,256]{1,0:T(8,128)S(1)}, f32[128,256]{1,0:T(8,128)S(1)}) custom-call(bf16[256,512]{1,0:T(8,128)(2,1)S(1)} %fusion.2.sent_ref, bf16[256,512]{1,0:T(8,128)(2,1)S(1)} %collective-permute-done.25.left_ref, bf16[2,256,512]{2,1,0:T(8,128)(2,1)S(1)} %get-tuple-element.34.mine_ref, ...), custom_call_target="tpu_custom_call" | custom-call | bytes 1000000 | tf_op jit(solution)/shard_map/pallas_call | solution.py:277
  81.0 3.8 %collective-permute-start.26 = (f32[128,256]{1,0:T(8,128)S(1)}, f32[128,256]{1,0:T(8,128)S(1)}, u32[]{:S(2)}, u32[]{:S(2)}) collective-permute-start(f32[128,256]{1,0:T(8,128)S(1)} %get-tuple-element.39), channel_id=1, source_target_pairs={{0,16},{16,0},{32,48},{48,32},{64,80},{80,64},{96,112},{112,96},{1... | collective-permute-start | bytes 393224 | tf_op jit(solution)/shard_map/ppermute | solution.py:39
  86.5 10.5 %all-to-all-start = ((f32[128,1,256]{2,1,0:T(1,128)}), f32[128,1,256]{2,1,0:T(1,128)S(1)}, u32[]{:S(2)}, u32[]{:S(2)}) async-start(f32[128,1,256]{2,1,0:T(1,128)} %copy.9), calls=%async_computation | async-start | bytes 262144 | tf_op jit(solution)/shard_map/all_to_all | solution.py:317
  97.1 1.3 %shard_map.91 = bf16[512,256]{1,0:T(8,128)(2,1)} custom-call(bf16[256,512]{1,0:T(8,128)(2,1)S(1)} %collective-permute-done.22.right_ref, bf16[256,512]{1,0:T(8,128)(2,1)S(1)} %collective-permute-done.25.left_ref, bf16[2,256,512]{2,1,0:T(8,128)(2,1)S(1)} %get-tuple-element.34.mine_ref, bf16[2,256,512]{2,1,0:T(8,128)(2,1)S(1)} %collective-permute-done.21.other_ref, ...), custom_call_target="tpu_custom_call" | custom-call | bytes 1000000 | tf_op jit(solution)/shard_map/pallas_call | solution.py:225
  98.4 9.8 %all-to-all-done = f32[128,1,256]{2,1,0:T(1,128)S(1)} async-done(((f32[128,1,256]{2,1,0:T(1,128)}), f32[128,1,256]{2,1,0:T(1,128)S(1)}, u32[]{:S(2)}, u32[]{:S(2)}) %all-to-all-start) | async-done | bytes 131104 | tf_op jit(solution)/shard_map/all_to_all | solution.py:317
  (53 shorter events, 8.5 us)
Async XLA Ops:
  1.7 9.6 %collective-permute-start.2 = (bf16[8,8192]{1,0:T(8,128)(2,1)S(1)}, bf16[8,8192]{1,0:T(8,128)(2,1)S(1)}, u32[]{:S(2)}, u32[]{:S(2)}) collective-permute-start(bf16[8,8192]{1,0:T(8,128)(2,1)S(1)} %get-tuple-element.47), channel_id=1, source_target_pairs={{0,1},{1,2},{2,3},{3,0},{4,5},{5,6},{6,7},{7,4},{8,9},{9,10},{10,1... | collective-permute-start | bytes 393224 | tf_op jit(solution)/shard_map/ppermute | solution.py:25
  3.8 8.6 %collective-permute-start.1 = (bf16[8,8192]{1,0:T(8,128)(2,1)S(1)}, bf16[8,8192]{1,0:T(8,128)(2,1)S(1)}, u32[]{:S(2)}, u32[]{:S(2)}) collective-permute-start(bf16[8,8192]{1,0:T(8,128)(2,1)S(1)} %get-tuple-element.47), channel_id=1, source_target_pairs={{0,2},{1,3},{2,0},{3,1},{4,6},{5,7},{6,4},{7,5},{8,10},{9,11},{10,... | collective-permute-start | bytes 393224 | tf_op jit(solution)/shard_map/ppermute | solution.py:25
  6.3 6.2 %collective-permute-start = (bf16[8,8192]{1,0:T(8,128)(2,1)S(1)}, bf16[8,8192]{1,0:T(8,128)(2,1)S(1)}, u32[]{:S(2)}, u32[]{:S(2)}) collective-permute-start(bf16[8,8192]{1,0:T(8,128)(2,1)S(1)} %get-tuple-element.47), channel_id=1, source_target_pairs={{0,3},{1,0},{2,1},{3,2},{4,7},{5,4},{6,5},{7,6},{8,11},{9,8},{10,9... | collective-permute-start | bytes 393224 | tf_op jit(solution)/shard_map/ppermute | solution.py:25
  7.4 5.4 %collective-permute-start.5 = (bf16[8,8192]{1,0:T(8,128)(2,1)S(1)}, bf16[8,8192]{1,0:T(8,128)(2,1)S(1)}, u32[]{:S(2)}, u32[]{:S(2)}) collective-permute-start(bf16[8,8192]{1,0:T(8,128)(2,1)S(1)} %get-tuple-element.46), channel_id=1, source_target_pairs={{0,4},{1,5},{2,6},{3,7},{4,8},{5,9},{6,10},{7,11},{8,12},{9,13},{1... | collective-permute-start | bytes 393224 | tf_op jit(solution)/shard_map/ppermute | solution.py:30
  8.7 7.1 %collective-permute-start.4 = (bf16[8,8192]{1,0:T(8,128)(2,1)S(1)}, bf16[8,8192]{1,0:T(8,128)(2,1)S(1)}, u32[]{:S(2)}, u32[]{:S(2)}) collective-permute-start(bf16[8,8192]{1,0:T(8,128)(2,1)S(1)} %get-tuple-element.46), channel_id=1, source_target_pairs={{0,8},{1,9},{2,10},{3,11},{4,12},{5,13},{6,14},{7,15},{8,0},{9,1},... | collective-permute-start | bytes 393224 | tf_op jit(solution)/shard_map/ppermute | solution.py:30
  11.4 5.1 %collective-permute-start.3 = (bf16[8,8192]{1,0:T(8,128)(2,1)S(1)}, bf16[8,8192]{1,0:T(8,128)(2,1)S(1)}, u32[]{:S(2)}, u32[]{:S(2)}) collective-permute-start(bf16[8,8192]{1,0:T(8,128)(2,1)S(1)} %get-tuple-element.46), channel_id=1, source_target_pairs={{0,12},{1,13},{2,14},{3,15},{4,0},{5,1},{6,2},{7,3},{8,4},{9,5},{1... | collective-permute-start | bytes 393224 | tf_op jit(solution)/shard_map/ppermute | solution.py:30
  16.5 12.3 %collective-permute-start.8 = (bf16[32,8192]{1,0:T(8,128)(2,1)S(1)}, bf16[32,8192]{1,0:T(8,128)(2,1)S(1)}, u32[]{:S(2)}, u32[]{:S(2)}) collective-permute-start(bf16[32,8192]{1,0:T(8,128)(2,1)S(1)} %pad_maximum_fusion.refs_0_), channel_id=1, source_target_pairs={{0,4},{1,5},{2,6},{3,7},{4,8},{5,9},{6,10},{7,11},{8,12},{9,13},{1... | collective-permute-start | bytes 1572872 | tf_op jit(solution)/shard_map/ppermute | solution.py:30
  16.7 12.2 %collective-permute-start.7 = (bf16[32,8192]{1,0:T(8,128)(2,1)S(1)}, bf16[32,8192]{1,0:T(8,128)(2,1)S(1)}, u32[]{:S(2)}, u32[]{:S(2)}) collective-permute-start(bf16[32,8192]{1,0:T(8,128)(2,1)S(1)} %pad_maximum_fusion.refs_0_), channel_id=1, source_target_pairs={{0,12},{1,13},{2,14},{3,15},{4,0},{5,1},{6,2},{7,3},{8,4},{9,5},{1... | collective-permute-start | bytes 1572872 | tf_op jit(solution)/shard_map/ppermute | solution.py:30
  19.3 12.4 %collective-permute-start.12 = (bf16[32,8192]{1,0:T(8,128)(2,1)S(1)}, bf16[32,8192]{1,0:T(8,128)(2,1)S(1)}, u32[]{:S(2)}, u32[]{:S(2)}) collective-permute-start(bf16[32,8192]{1,0:T(8,128)(2,1)S(1)} %pad_maximum_fusion.1.refs_5_), channel_id=1, source_target_pairs={{0,1},{1,2},{2,3},{3,0},{4,5},{5,6},{6,7},{7,4},{8,9},{9,10},{10,1... | collective-permute-start | bytes 1572872 | tf_op jit(solution)/shard_map/ppermute | solution.py:25
  19.6 12.7 %collective-permute-start.11 = (bf16[32,8192]{1,0:T(8,128)(2,1)S(1)}, bf16[32,8192]{1,0:T(8,128)(2,1)S(1)}, u32[]{:S(2)}, u32[]{:S(2)}) collective-permute-start(bf16[32,8192]{1,0:T(8,128)(2,1)S(1)} %pad_maximum_fusion.1.refs_5_), channel_id=1, source_target_pairs={{0,3},{1,0},{2,1},{3,2},{4,7},{5,4},{6,5},{7,6},{8,11},{9,8},{10,9... | collective-permute-start | bytes 1572872 | tf_op jit(solution)/shard_map/ppermute | solution.py:25
  21.9 18.0 %collective-permute-start.6 = (bf16[512,256]{1,0:T(8,128)(2,1)}, bf16[512,256]{1,0:T(8,128)(2,1)S(1)}, u32[]{:S(2)}, u32[]{:S(2)}) collective-permute-start(bf16[512,256]{1,0:T(8,128)(2,1)} %feat_ref.1), channel_id=1, source_target_pairs={{0,224},{16,240},{32,0},{48,16},{64,32},{80,48},{96,64},{112,80},{... | collective-permute-start | bytes 786440 | tf_op jit(solution)/shard_map/ppermute | solution.py:35
  28.8 11.1 %collective-permute-start.9 = (bf16[16,8192]{1,0:T(8,128)(2,1)S(1)}, bf16[16,8192]{1,0:T(8,128)(2,1)S(1)}, u32[]{:S(2)}, u32[]{:S(2)}) collective-permute-start(bf16[16,8192]{1,0:T(8,128)(2,1)S(1)} %slice.82), channel_id=1, source_target_pairs={{0,4},{1,5},{2,6},{3,7},{4,8},{5,9},{6,10},{7,11},{8,12},{9,13},{1... | collective-permute-start | bytes 786440 | tf_op jit(solution)/shard_map/ppermute | solution.py:30
  28.9 11.0 %collective-permute-start.10 = (bf16[16,8192]{1,0:T(8,128)(2,1)S(1)}, bf16[16,8192]{1,0:T(8,128)(2,1)S(1)}, u32[]{:S(2)}, u32[]{:S(2)}) collective-permute-start(bf16[16,8192]{1,0:T(8,128)(2,1)S(1)} %slice.83), channel_id=1, source_target_pairs={{0,12},{1,13},{2,14},{3,15},{4,0},{5,1},{6,2},{7,3},{8,4},{9,5},{1... | collective-permute-start | bytes 786440 | tf_op jit(solution)/shard_map/ppermute | solution.py:30
  31.7 8.2 %collective-permute-start.13 = (bf16[16,8192]{1,0:T(8,128)(2,1)S(1)}, bf16[16,8192]{1,0:T(8,128)(2,1)S(1)}, u32[]{:S(2)}, u32[]{:S(2)}) collective-permute-start(bf16[16,8192]{1,0:T(8,128)(2,1)S(1)} %slice.84), channel_id=1, source_target_pairs={{0,1},{1,2},{2,3},{3,0},{4,5},{5,6},{6,7},{7,4},{8,9},{9,10},{10,1... | collective-permute-start | bytes 786440 | tf_op jit(solution)/shard_map/ppermute | solution.py:25
  32.3 7.6 %collective-permute-start.14 = (bf16[16,8192]{1,0:T(8,128)(2,1)S(1)}, bf16[16,8192]{1,0:T(8,128)(2,1)S(1)}, u32[]{:S(2)}, u32[]{:S(2)}) collective-permute-start(bf16[16,8192]{1,0:T(8,128)(2,1)S(1)} %slice.85), channel_id=1, source_target_pairs={{0,3},{1,0},{2,1},{3,2},{4,7},{5,4},{6,5},{7,6},{8,11},{9,8},{10,9... | collective-permute-start | bytes 786440 | tf_op jit(solution)/shard_map/ppermute | solution.py:25
  35.2 0.7 copy-start.2
  42.6 7.6 %collective-permute-start.15 = (bf16[2,256,512]{2,1,0:T(8,128)(2,1)S(1)}, bf16[2,256,512]{2,1,0:T(8,128)(2,1)S(1)}, u32[]{:S(2)}, u32[]{:S(2)}) collective-permute-start(bf16[2,256,512]{2,1,0:T(8,128)(2,1)S(1)} %get-tuple-element.29), channel_id=1, source_target_pairs={{0,16},{16,0},{32,48},{48,32},{64,80},{80,64},{96,112},{112,96},{1... | collective-permute-start | bytes 1572872 | tf_op jit(solution)/shard_map/ppermute | solution.py:39
  50.0 9.4 %collective-permute-start.17 = (bf16[2,256,512]{2,1,0:T(8,128)(2,1)S(1)}, bf16[2,256,512]{2,1,0:T(8,128)(2,1)S(1)}, u32[]{:S(2)}, u32[]{:S(2)}) collective-permute-start(bf16[2,256,512]{2,1,0:T(8,128)(2,1)S(1)} %get-tuple-element.31), channel_id=1, source_target_pairs={{0,16},{16,0},{32,48},{48,32},{64,80},{80,64},{96,112},{112,96},{1... | collective-permute-start | bytes 1572872 | tf_op jit(solution)/shard_map/ppermute | solution.py:39
  50.3 11.3 %collective-permute-start.23 = (bf16[256,512]{1,0:T(8,128)(2,1)S(1)}, bf16[256,512]{1,0:T(8,128)(2,1)S(1)}, u32[]{:S(2)}, u32[]{:S(2)}) collective-permute-start(bf16[256,512]{1,0:T(8,128)(2,1)S(1)} %get-tuple-element.44), channel_id=1, source_target_pairs={{0,224},{16,240},{32,0},{48,16},{64,32},{80,48},{96,64},{112,80},{... | collective-permute-start | bytes 786440 | tf_op jit(solution)/shard_map/ppermute | solution.py:35
  56.4 8.3 %collective-permute-start.16 = (bf16[256,512]{1,0:T(8,128)(2,1)S(1)}, bf16[256,512]{1,0:T(8,128)(2,1)S(1)}, u32[]{:S(2)}, u32[]{:S(2)}) collective-permute-start(bf16[256,512]{1,0:T(8,128)(2,1)S(1)} %get-tuple-element.45), channel_id=1, source_target_pairs={{0,32},{16,48},{32,64},{48,80},{64,96},{80,112},{96,128},{112,144}... | collective-permute-start | bytes 786440 | tf_op jit(solution)/shard_map/ppermute | solution.py:35
  59.3 20.5 %copy-start = (bf16[512,256]{1,0:T(8,128)(2,1)S(1)}, bf16[512,256]{1,0:T(8,128)(2,1)}, u32[]{:S(2)}) copy-start(bf16[512,256]{1,0:T(8,128)(2,1)} %feat_ref.1) | copy-start | bytes 786436
  59.3 11.3 %collective-permute-start.19 = (bf16[2,256,512]{2,1,0:T(8,128)(2,1)S(1)}, bf16[2,256,512]{2,1,0:T(8,128)(2,1)S(1)}, u32[]{:S(2)}, u32[]{:S(2)}) collective-permute-start(bf16[2,256,512]{2,1,0:T(8,128)(2,1)S(1)} %get-tuple-element.33), channel_id=1, source_target_pairs={{0,16},{16,0},{32,48},{48,32},{64,80},{80,64},{96,112},{112,96},{1... | collective-permute-start | bytes 1572872 | tf_op jit(solution)/shard_map/ppermute | solution.py:39
  64.9 6.2 %collective-permute-start.24 = (bf16[256,512]{1,0:T(8,128)(2,1)S(1)}, bf16[256,512]{1,0:T(8,128)(2,1)S(1)}, u32[]{:S(2)}, u32[]{:S(2)}) collective-permute-start(bf16[256,512]{1,0:T(8,128)(2,1)S(1)} %get-tuple-element.42), channel_id=1, source_target_pairs={{0,224},{16,240},{32,0},{48,16},{64,32},{80,48},{96,64},{112,80},{... | collective-permute-start | bytes 786440 | tf_op jit(solution)/shard_map/ppermute | solution.py:35
  65.5 31.5 %copy-start.1 = (bf16[256,256]{1,0:T(8,128)(2,1)S(1)}, bf16[256,256]{1,0:T(8,128)(2,1)}, u32[]{:S(2)}) copy-start(bf16[256,256]{1,0:T(8,128)(2,1)} %weight_ref.1) | copy-start | bytes 393220
  65.5 7.4 %collective-permute-start.18 = (bf16[256,512]{1,0:T(8,128)(2,1)S(1)}, bf16[256,512]{1,0:T(8,128)(2,1)S(1)}, u32[]{:S(2)}, u32[]{:S(2)}) collective-permute-start(bf16[256,512]{1,0:T(8,128)(2,1)S(1)} %get-tuple-element.43), channel_id=1, source_target_pairs={{0,32},{16,48},{32,64},{48,80},{64,96},{80,112},{96,128},{112,144}... | collective-permute-start | bytes 786440 | tf_op jit(solution)/shard_map/ppermute | solution.py:35
  68.9 7.0 %collective-permute-start.21 = (bf16[2,256,512]{2,1,0:T(8,128)(2,1)S(1)}, bf16[2,256,512]{2,1,0:T(8,128)(2,1)S(1)}, u32[]{:S(2)}, u32[]{:S(2)}) collective-permute-start(bf16[2,256,512]{2,1,0:T(8,128)(2,1)S(1)} %get-tuple-element.35), channel_id=1, source_target_pairs={{0,16},{16,0},{32,48},{48,32},{64,80},{80,64},{96,112},{112,96},{1... | collective-permute-start | bytes 1572872 | tf_op jit(solution)/shard_map/ppermute | solution.py:39
  73.1 6.5 %collective-permute-start.20 = (bf16[256,512]{1,0:T(8,128)(2,1)S(1)}, bf16[256,512]{1,0:T(8,128)(2,1)S(1)}, u32[]{:S(2)}, u32[]{:S(2)}) collective-permute-start(bf16[256,512]{1,0:T(8,128)(2,1)S(1)} %get-tuple-element.41), channel_id=1, source_target_pairs={{0,32},{16,48},{32,64},{48,80},{64,96},{80,112},{96,128},{112,144}... | collective-permute-start | bytes 786440 | tf_op jit(solution)/shard_map/ppermute | solution.py:35
  73.2 6.5 %collective-permute-start.25 = (bf16[256,512]{1,0:T(8,128)(2,1)S(1)}, bf16[256,512]{1,0:T(8,128)(2,1)S(1)}, u32[]{:S(2)}, u32[]{:S(2)}) collective-permute-start(bf16[256,512]{1,0:T(8,128)(2,1)S(1)} %get-tuple-element.40), channel_id=1, source_target_pairs={{0,224},{16,240},{32,0},{48,16},{64,32},{80,48},{96,64},{112,80},{... | collective-permute-start | bytes 786440 | tf_op jit(solution)/shard_map/ppermute | solution.py:35
  81.0 4.8 %collective-permute-start.26 = (f32[128,256]{1,0:T(8,128)S(1)}, f32[128,256]{1,0:T(8,128)S(1)}, u32[]{:S(2)}, u32[]{:S(2)}) collective-permute-start(f32[128,256]{1,0:T(8,128)S(1)} %get-tuple-element.39), channel_id=1, source_target_pairs={{0,16},{16,0},{32,48},{48,32},{64,80},{80,64},{96,112},{112,96},{1... | collective-permute-start | bytes 393224 | tf_op jit(solution)/shard_map/ppermute | solution.py:39
  84.7 12.3 %collective-permute-start.22 = (bf16[256,512]{1,0:T(8,128)(2,1)S(1)}, bf16[256,512]{1,0:T(8,128)(2,1)S(1)}, u32[]{:S(2)}, u32[]{:S(2)}) collective-permute-start(bf16[256,512]{1,0:T(8,128)(2,1)S(1)} %fusion.2.sent_ref), channel_id=1, source_target_pairs={{0,32},{16,48},{32,64},{48,80},{64,96},{80,112},{96,128},{112,144}... | collective-permute-start | bytes 786440 | tf_op jit(solution)/shard_map/ppermute | solution.py:35
  86.5 21.7 %all-to-all-start = ((f32[128,1,256]{2,1,0:T(1,128)}), f32[128,1,256]{2,1,0:T(1,128)S(1)}, u32[]{:S(2)}, u32[]{:S(2)}) async-start(f32[128,1,256]{2,1,0:T(1,128)} %copy.9), calls=%async_computation | async-start | bytes 262144 | tf_op jit(solution)/shard_map/all_to_all | solution.py:317
